TPU v7x, 128 devices: a whole 4x4x4 slice. The times are simulated.
128 devices in a mesh: band: 16 (over y, z), shard: 8 (over x, core).
Axes of the slice: x: 4, y: 4, z: 4, core: 2. Of those that a mesh axis runs over, the one named last changes fastest.
Arguments:
- grid_input: bfloat16 [1024, 512, 474], P('band', 'shard'), may hold values from -6 to 6
- w_stem: bfloat16 [9, 474, 512], replicated, may hold values from -0.09375 to 0.09375
- b_stem: float32 [512], replicated, may hold values from -3 to 3
- w_edge: bfloat16 [512, 512], replicated, may hold values from -0.25 to 0.25
- w_node: bfloat16 [512, 512], replicated, may hold values from -0.25 to 0.25
- src_index: int32 [128, 128, 16], P(('band', 'shard')), may hold values from 0 to 1023
- dst_index: int32 [128, 128, 16], P(('band', 'shard')), may hold values from 0 to 319
- counts: int32 [128, 128], P(('band', 'shard')), may hold values from 0 to 16, as said below
- mesh_cotangent: bfloat16 [40960, 512], P(('band', 'shard')), may hold values from -0.119628906 to 0.119628906
Outputs:
- mesh_out: bfloat16 [40960, 512], P(('band', 'shard'))
- grad_stem: float32 [9, 474, 512], replicated
- grad_bias: float32 [512], replicated
- grad_edge: float32 [512, 512], replicated
- grad_node: float32 [512, 512], replicated
Inputs may be any that keep to these rules, and one draw needn't show every extreme that they name: counts[q, r] of the 16 slots of each block are used; 16 is reached, and some destination owner receives 16 from every sender.
All inputs are finite; a program needn't handle non-finite values.
Results may differ from a plain program's by a relative error of at most 0.0066.
Values may be sent and summed in bfloat16 or wider, within the bound.
No kernel may reach another device: no remote copies, remote signals or barrier semaphores. Data moves between devices by JAX's collectives and lax.ppermute only.
A program may use at most 128 MiB of HBM per device.

v0:
```python
import functools
import itertools

import jax
import jax.numpy as jnp
from jax import lax
from jax.experimental import pallas as pl
from jax.experimental.pallas import tpu as pltpu
from jax.sharding import Mesh, PartitionSpec as P

EVERY = ("band", "chip", "core")
TAPS = 9
LINE = 4
MIB = 1024 * 1024
TILE = 256


def f32_dot(first, second):
    return jnp.dot(first, second, preferred_element_type=jnp.float32)


def inner_dot(first, second):
    return lax.dot_general(
        first, second, (((0,), (0,)), ((), ())), preferred_element_type=jnp.float32
    )


def right_dot(first, second):
    return lax.dot_general(
        first, second, (((1,), (1,)), ((), ())), preferred_element_type=jnp.float32
    )


def core_swap(array):
    return lax.ppermute(array, "core", [(0, 1), (1, 0)])


def device_number(y, z, x, core):
    return ((y * LINE + z) * LINE + x) * 2 + core


def line_pairs(step):
    pairs = []
    for y, z, x in itertools.product(range(LINE), repeat=3):
        pairs.append((device_number(y, z, x, 0), device_number(y, z, (x + step) % LINE, 0)))
        pairs.append((device_number(y, z, x, 1), device_number((y + step) % LINE, z, x, 1)))
    return pairs


def plane_groups():
    planes = []
    for fixed in range(LINE):
        rest = list(itertools.product(range(LINE), repeat=2))
        planes.append([device_number(y, z, fixed, 0) for y, z in rest])
        planes.append([device_number(fixed, z, x, 1) for x, z in rest])
    return planes


def whole(memory=pltpu.VMEM):
    return pl.BlockSpec(memory_space=memory)


def params(mib):
    return pltpu.CompilerParams(vmem_limit_bytes=mib * MIB)


def cost(flops, moved):
    return pl.CostEstimate(flops=int(flops), bytes_accessed=int(moved), transcendentals=0)


def rows_at(number, size=TILE):
    return pl.ds(pl.multiple_of(number * size, size), size)


def unrolled(count):
    return pl.loop(0, count, unroll=True)


def column_picker(image_rows, cols, parts):
    half = cols // 2
    shape = (3 * image_rows * half, image_rows * cols)
    out = lax.broadcasted_iota(jnp.int32, shape, 0)
    inside = lax.broadcasted_iota(jnp.int32, shape, 1)
    per_tap = image_rows * half
    tap = out // per_tap
    rest = out - tap * per_tap
    line = rest // half
    col = 2 * (rest - line * half) + tap - 1
    if parts == 2:
        pairs = image_rows // 2
        parity = line // pairs
        line = 2 * (line - parity * pairs) + parity
    hit = (col >= 0) & (inside == line * cols + col)
    return jnp.where(hit, 1.0, 0.0).astype(jnp.bfloat16)


def stem_kernel(
    west_ref, north_ref, corner_ref, picker_ref, north_picker_ref, bias_ref, source_ref,
    grid_hbm, w_hbm, even_hbm, odd_hbm, slope_hbm, out_hbm,
    grid, raw, weights, even, odd, latent, slope, out, in_sems, w_sems, out_sems, slope_sems, row_sems,
):
    rows, cols, channels = grid.shape
    half_rows, half_cols = rows // 2, cols // 2
    width = even.shape[-1]
    chunks = in_sems.shape[0]
    per_chunk = rows // chunks
    bf16 = jnp.bfloat16

    loads = [
        pltpu.make_async_copy(
            grid_hbm.at[rows_at(chunk, per_chunk)], grid.at[rows_at(chunk, per_chunk)], in_sems.at[chunk]
        )
        for chunk in range(chunks)
    ]
    w_loads = [
        pltpu.make_async_copy(w_hbm.at[tap], raw.at[tap], w_sems.at[tap]) for tap in range(TAPS)
    ]
    for copy in loads:
        copy.start()

    tail = width - 128
    even[:, :, :, tail:] = jnp.zeros((3, half_rows, half_cols, 128), bf16)
    odd[:, :, :, tail:] = jnp.zeros((3, half_rows + 1, half_cols, 128), bf16)
    gap = channels // 16 * 16
    for tap in range(TAPS):
        weights[tap * width + gap : (tap + 1) * width] = jnp.zeros((width - gap, width), bf16)
    north = f32_dot(north_picker_ref[...], north_ref[0]).astype(bf16)
    for tap in range(3):
        odd[tap, 0, :, :channels] = north[tap * half_cols : (tap + 1) * half_cols]

    for chunk in range(chunks):
        loads[chunk].wait()
        if chunk == chunks - 2:
            for copy in w_loads:
                copy.start()

        @unrolled(per_chunk // 4)
        def _(step):
            group = chunk * (per_chunk // 4) + step
            block = grid[pl.ds(4 * group, 4)].reshape(4 * cols, channels)
            picked = f32_dot(picker_ref[...], block).astype(bf16)
            picked = picked.reshape(3, 2, 2, half_cols, channels)
            for tap in range(3):
                even[tap, pl.ds(2 * group, 2), :, :channels] = picked[tap, 0]
                odd[tap, pl.ds(2 * group + 1, 2), :, :channels] = picked[tap, 1]

    def patch(target, first, count, column):
        old = target[0, first : first + count, 0:16, :channels].astype(jnp.float32)
        line = lax.broadcasted_iota(jnp.int32, old.shape, 1)
        new = jnp.where(line == 0, column.astype(jnp.float32), old)
        target[0, first : first + count, 0:16, :channels] = new.astype(bf16)

    patch(even, 0, half_rows, west_ref[:, 0])
    patch(odd, 1, half_rows, west_ref[:, 1])
    patch(odd, 0, 1, corner_ref[...])
    phase_copies = [
        pltpu.make_async_copy(even, even_hbm, out_sems.at[0]),
        pltpu.make_async_copy(odd, odd_hbm, out_sems.at[1]),
    ]
    for tap in range(TAPS):
        w_loads[tap].wait()
        weights[tap * width : tap * width + channels] = raw[tap]
    for copy in phase_copies:
        copy.start()

    tile_rows = TILE // half_cols
    points = latent.shape[0]

    def slope_copy(step):
        here = rows_at(step)
        return pltpu.make_async_copy(slope.at[here], slope_hbm.at[here], slope_sems.at[step])

    def row_copy(step):
        here = rows_at(step)
        return pltpu.make_async_copy(out.at[here], out_hbm.at[here], row_sems.at[step])

    @unrolled(points // TILE)
    def _(step):
        pieces = []
        for row_tap in range(3):
            for col_tap in range(3):
                first = step * tile_rows + (row_tap // 2)
                held = even if row_tap == 1 else odd
                pieces.append(held[col_tap, pl.ds(first, tile_rows)].reshape(TILE, width))
        pre = f32_dot(jnp.concatenate(pieces, axis=1), weights[...]) + bias_ref[...]
        sigmoid = jax.nn.sigmoid(pre)
        here = rows_at(step)
        slope[here] = sigmoid * (1.0 + pre * (1.0 - sigmoid))
        latent[here] = (pre * sigmoid).astype(bf16)
        slope_copy(step).start()

    @unrolled(out.shape[0] // TILE)
    def _(step):
        here = rows_at(step)
        point = lax.broadcasted_iota(jnp.int32, (TILE, points), 1)
        pick = jnp.where(point == source_ref[here], 1.0, 0.0).astype(bf16)
        out[here] = f32_dot(pick, latent[...]).astype(bf16)
        row_copy(step).start()

    for copy in phase_copies:
        copy.wait()

    @pl.loop(0, points // TILE)
    def _(step):
        slope_copy(step).wait()

    @pl.loop(0, out.shape[0] // TILE)
    def _(step):
        row_copy(step).wait()


def flip_kernel(channels, even_ref, odd_ref, out_ref):
    number = pl.program_id(0)
    row_tap = number // 3
    col_tap = number % 3
    half_rows, half_cols, width = even_ref.shape[1:]

    def write(values):
        flipped = values.reshape(half_rows * half_cols, width).T
        line = lax.broadcasted_iota(jnp.int32, flipped.shape, 0)
        ones = (line == channels) & (number == 0)
        out_ref[0] = jnp.where(ones, 1.0, flipped.astype(jnp.float32)).astype(jnp.bfloat16)

    @pl.when(row_tap == 1)
    def _():
        write(even_ref[col_tap])

    @pl.when(row_tap != 1)
    def _():
        write(odd_ref[col_tap, pl.ds(row_tap // 2, half_rows)])


def edge_kernel(side, w_ref, flipped_ref, dst_ref, agg_ref, rows_hbm, *refs):
    outs = 2 if side else 1
    placed, (rows, *kept), (in_sems, out_sems) = refs[:outs], refs[outs : 2 * outs + 1], refs[2 * outs + 1 :]
    nodes = agg_ref.shape[0]
    tiles = in_sems.shape[0]
    tile = rows.shape[0] // tiles
    bf16 = jnp.bfloat16

    def load(step):
        here = rows_at(step, tile)
        return pltpu.make_async_copy(rows_hbm.at[here], rows.at[here], in_sems.at[step])

    def stores(step):
        here = rows_at(step, tile)
        return [
            pltpu.make_async_copy(kept[i].at[here], placed[i].at[here], out_sems.at[i, step])
            for i in range(outs)
        ]

    load(0).start()

    @unrolled(tiles)
    def _(step):
        here = rows_at(step, tile)
        node = lax.broadcasted_iota(jnp.int32, (tile, nodes), 1)
        pick = jnp.where(node == dst_ref[here], 1.0, 0.0).astype(bf16)
        grad_msg = f32_dot(pick, agg_ref[...])
        load(step).wait()

        @pl.when(step + 1 < tiles)
        def _():
            load(step + 1).start()

        pre = f32_dot(rows[here], w_ref[...])
        sigmoid = jax.nn.sigmoid(pre)
        grad_pre = (grad_msg * (sigmoid * (1.0 + pre * (1.0 - sigmoid)))).astype(bf16)
        if side:
            kept[0][here] = (pre * sigmoid).astype(bf16)
            kept[1][here] = grad_pre
        else:
            kept[0][here] = f32_dot(grad_pre, flipped_ref[...]).astype(bf16)
        for copy in stores(step):
            copy.start()

    for step in range(tiles):
        for copy in stores(step):
            copy.wait()


def quarter_of(spot, step):
    return lax.rem(spot + step + LINE, LINE)


def gradients_kernel(
    where_ref, source_ref, returned_hbm, slope_hbm, edge_hbm, node_hbm, patches_hbm,
    sent_line_hbm, sent_own_hbm, kept_line_hbm, kept_own_hbm,
    returned, slope, stemout, patches, smalls, out, before_sems, patch_sems, small_sems, out_sems,
):
    half_width = out.shape[3]
    depth = out.shape[2] // LINE
    points, width = stemout.shape
    slots = returned.shape[0]
    bf16 = jnp.bfloat16
    before = [
        pltpu.make_async_copy(returned_hbm, returned, before_sems.at[0]),
        pltpu.make_async_copy(slope_hbm, slope, before_sems.at[1]),
    ]
    patch_loads = [
        pltpu.make_async_copy(patches_hbm.at[tap], patches.at[tap], patch_sems.at[tap])
        for tap in range(TAPS)
    ]
    small_loads = [
        pltpu.make_async_copy(placed, smalls.at[number], small_sems.at[number])
        for number, placed in enumerate((edge_hbm, node_hbm))
    ]
    placed = ((sent_line_hbm, sent_own_hbm), (kept_line_hbm, kept_own_hbm))

    def stores(part):
        copies = []
        for slot in range(LINE):
            quarter = quarter_of(where_ref[3 - part], slot + 1)
            target = placed[part][0].at[slot] if slot < LINE - 1 else placed[part][1]
            copies.append(
                pltpu.make_async_copy(out.at[part, :, pl.ds(pl.multiple_of(quarter * depth, depth), depth)], target, out_sems.at[part, slot])
            )
        return copies

    def finish(block, part, values):
        out[part, block] = values.astype(bf16)

    def columns(part):
        return pl.ds(pl.multiple_of(where_ref[1 - part] * half_width, half_width), half_width)

    for copy in before:
        copy.start()
    for copy in before:
        copy.wait()
    for copy in patch_loads + small_loads:
        copy.start()

    @unrolled(points // TILE)
    def _(tile):
        here = rows_at(tile)
        point = lax.broadcasted_iota(jnp.int32, (TILE, slots), 0) + tile * TILE
        pick = jnp.where(point == source_ref[...], 1.0, 0.0).astype(bf16)
        grad_latent = f32_dot(pick, returned[...])
        stemout[here] = (grad_latent * slope[here]).astype(bf16)

    for part in range(2):
        for tap in range(TAPS):
            if part == 0 and tap in (0, TAPS // 2):
                for copy in patch_loads[tap : TAPS // 2 if tap == 0 else TAPS]:
                    copy.wait()
            finish(tap, part, f32_dot(patches[tap], stemout[:, columns(part)]))
        for number in range(2):
            if part == 0:
                small_loads[number].wait()
            finish(TAPS + number, part, smalls[number, :, columns(part)])
        for copy in stores(part):
            copy.start()
    for part in range(2):
        for copy in stores(part):
            copy.wait()


def line_sum_kernel(kept_ref, received_ref, one_ref, two_ref, three_ref, out_ref):
    for piece in range(out_ref.shape[0]):
        here = (slice(None), pl.ds(piece // 2 * 16, 16), pl.ds(piece % 2 * 128, 128))
        total = kept_ref[here].astype(jnp.float32)
        for ref in (received_ref, one_ref, two_ref, three_ref):
            total = total + ref[here].astype(jnp.float32)
        out_ref[piece] = total.astype(out_ref.dtype)


def final_kernel(steps, where_ref, *refs):
    held = refs[: 2 * len(steps)]
    stem_hbm, bias_hbm, edge_hbm, node_hbm, blocks, last, bias, stem_sems, small_sems, bias_sems = refs[-10:]
    channels = stem_hbm.shape[1]
    depth, half_width = blocks.shape[2:]
    full = channels // depth
    spare = channels - full * depth
    finish = []
    for index, ref in enumerate(held):
        part = index % 2
        quarter = quarter_of(where_ref[2 + part], -steps[index // 2])
        half = where_ref[part]
        rows = pl.ds(pl.multiple_of(quarter * depth, depth), depth)
        columns = pl.ds(pl.multiple_of(half * half_width, half_width), half_width)
        for piece in range(ref.shape[0]):
            row, lane = piece // 2 * 16, piece % 2 * 128
            blocks[index, :, row : row + 16, lane : lane + 128] = ref[piece].astype(jnp.float32)
        whole_copy = pltpu.make_async_copy(
            blocks.at[index, pl.ds(0, TAPS)], stem_hbm.at[:, rows, columns], stem_sems.at[index]
        )
        last_copy = pltpu.make_async_copy(
            last.at[part], stem_hbm.at[:, pl.ds(full * depth, spare), columns], stem_sems.at[index]
        )
        bias_copy = pltpu.make_async_copy(bias.at[part], bias_hbm.at[:, columns], bias_sems.at[index])
        small_copies = [
            pltpu.make_async_copy(
                blocks.at[index, TAPS + number], placed.at[rows, columns], small_sems.at[index, number]
            )
            for number, placed in enumerate((edge_hbm, node_hbm))
        ]

        @pl.when(quarter < full)
        def _():
            whole_copy.start()

        @pl.when(quarter == full)
        def _():
            last[part] = blocks[index, :TAPS, :spare]
            bias[part] = blocks[index, 0, spare : spare + 1]
            last_copy.start()
            bias_copy.start()

        for copy in small_copies:
            copy.start()
        finish.append((quarter, whole_copy, last_copy, bias_copy, small_copies))
    for quarter, whole_copy, last_copy, bias_copy, small_copies in finish:
        @pl.when(quarter < full)
        def _():
            whole_copy.wait()

        @pl.when(quarter == full)
        def _():
            last_copy.wait()
            bias_copy.wait()

        for copy in small_copies:
            copy.wait()


def shards(
    grid_input, w_stem, b_stem, w_edge, w_node, src_index, dst_index, counts, mesh_cotangent
):
    rows_here, cols_here, channels = grid_input.shape
    width = w_edge.shape[0]
    bands = lax.axis_size("band")
    columns = lax.axis_size("chip") * 2
    chips = bands * lax.axis_size("chip")
    core = lax.axis_index("core")
    device_count = 2 * chips
    slot_count = src_index.shape[2]
    slots = device_count * slot_count
    half_rows = rows_here // 2
    half_cols = cols_here // 2
    points = half_rows * half_cols
    half_width = width // 2
    node_total = mesh_cotangent.shape[0]
    bf16, f32 = jnp.bfloat16, jnp.float32

    west = lax.ppermute(
        grid_input[:, -1:, :], ("chip", "core"), [(i, (i + 1) % columns) for i in range(columns)]
    )
    north = lax.ppermute(grid_input[-1:], "band", [(i, i + 1) for i in range(bands - 1)])
    corner = lax.ppermute(
        grid_input[-1:, -1:],
        EVERY,
        [
            (i * columns + j, (i + 1) * columns + (j + 1) % columns)
            for i in range(bands - 1)
            for j in range(columns)
        ],
    )
    flat_src = src_index.reshape(device_count, slot_count)
    slot_live = jnp.arange(slot_count, dtype=jnp.int32)[None, :] < counts.reshape(device_count, 1)
    source = jnp.where(slot_live, flat_src, -1)

    steps = slots // TILE
    even, odd, slope, outgoing = pl.pallas_call(
        stem_kernel,
        out_shape=(
            pltpu.HBM((3, half_rows, half_cols, width), bf16),
            pltpu.HBM((3, half_rows + 1, half_cols, width), bf16),
            pltpu.HBM((points, width), f32),
            pltpu.HBM((slots, width), bf16),
        ),
        in_specs=[whole()] * 7 + [whole(pltpu.HBM)] * 2,
        out_specs=(whole(pltpu.HBM),) * 4,
        scratch_shapes=[
            pltpu.VMEM((rows_here, cols_here, channels), bf16),
            pltpu.VMEM((TAPS, channels, width), bf16),
            pltpu.VMEM((TAPS * width, width), bf16),
            pltpu.VMEM((3, half_rows, half_cols, width), bf16),
            pltpu.VMEM((3, half_rows + 1, half_cols, width), bf16),
            pltpu.VMEM((points, width), bf16),
            pltpu.VMEM((points, width), f32),
            pltpu.VMEM((slots, width), bf16),
            pltpu.SemaphoreType.DMA((4,)),
            pltpu.SemaphoreType.DMA((TAPS,)),
            pltpu.SemaphoreType.DMA((2,)),
            pltpu.SemaphoreType.DMA((points // TILE,)),
            pltpu.SemaphoreType.DMA((steps,)),
        ],
        compiler_params=params(56),
        name="stem",
    )(
        west.reshape(half_rows, 2, 1, channels),
        north,
        corner,
        column_picker(4, cols_here, 2),
        column_picker(1, cols_here, 1),
        b_stem.reshape(1, width),
        source.reshape(slots, 1),
        grid_input,
        w_stem,
    )

    incoming = lax.all_to_all(
        outgoing.reshape(device_count, slot_count, width), EVERY, split_axis=0, concat_axis=0, tiled=True
    )
    arrived = incoming.reshape(slots, width)

    patches = pl.pallas_call(
        functools.partial(flip_kernel, channels),
        grid=(TAPS,),
        out_shape=pltpu.HBM((TAPS, width, points), bf16),
        in_specs=[
            pl.BlockSpec((3, half_rows, half_cols, width), lambda t: (0, 0, 0, 0)),
            pl.BlockSpec((3, half_rows + 1, half_cols, width), lambda t: (0, 0, 0, 0)),
        ],
        out_specs=pl.BlockSpec((1, width, points), lambda t: (t, 0, 0)),
        compiler_params=params(56),
        cost_estimate=cost(0, 16 * MIB),
        name="flip",
    )(even, odd)
    grad_agg = right_dot(mesh_cotangent, w_node).astype(bf16)
    dst_flat = dst_index.reshape(slots)

    dst_column = dst_flat.reshape(slots, 1)
    w_flipped = w_edge.T

    def edge_call(side):
        outs = 2 if side else 1
        return pl.pallas_call(
            functools.partial(edge_kernel, side),
            out_shape=(pltpu.HBM((slots, width), bf16),) * outs,
            in_specs=[whole()] * 4 + [whole(pltpu.HBM)],
            out_specs=(whole(pltpu.HBM),) * outs,
            scratch_shapes=[pltpu.VMEM((slots, width), bf16)] * (1 + outs)
            + [pltpu.SemaphoreType.DMA((2,)), pltpu.SemaphoreType.DMA((outs, 2))],
            compiler_params=params(40),
            cost_estimate=cost(4 * slots * width * width, 8 * MIB),
            name="edge_side" if side else "edge_back",
        )(w_edge, w_flipped, dst_column, grad_agg, arrived)

    (back,) = edge_call(False)

    returned = lax.all_to_all(
        back.reshape(device_count, slot_count, width), EVERY, split_axis=0, concat_axis=0, tiled=True
    ).reshape(slots, width)

    messages, grad_pre = edge_call(True)
    node_ids = jnp.arange(node_total, dtype=jnp.int32)
    onehot = (node_ids[:, None] == dst_flat[None, :]).astype(bf16)
    aggregate = f32_dot(onehot, messages).astype(bf16)
    mesh_out = f32_dot(aggregate, w_node).astype(bf16)
    grad_node = inner_dot(aggregate, mesh_cotangent).astype(bf16)
    grad_edge = inner_dot(arrived, grad_pre).astype(bf16)
    mesh_out, grad_edge, grad_node = lax.optimization_barrier((mesh_out, grad_edge, grad_node))

    blocks = TAPS + 2
    band, chip = lax.axis_index("band"), lax.axis_index("chip")
    up = band // LINE
    where = jnp.where(
        core == 0, jnp.stack([core, 1 - core, chip, up]), jnp.stack([core, 1 - core, up, chip])
    )
    depth = width // LINE
    source_row = source.reshape(1, slots)
    quarter_shape = (blocks, depth, half_width)
    line_shape = jax.ShapeDtypeStruct((LINE - 1,) + quarter_shape, bf16)
    own_shape = jax.ShapeDtypeStruct(quarter_shape, bf16)
    sent, sent_own, kept, kept_own = pl.pallas_call(
        gradients_kernel,
        out_shape=(line_shape, own_shape) * 2,
        in_specs=[whole(pltpu.SMEM), whole()] + [whole(pltpu.HBM)] * 5,
        out_specs=(whole(pl.ANY),) * 4,
        scratch_shapes=[
            pltpu.VMEM((slots, width), bf16),
            pltpu.VMEM((points, width), f32),
            pltpu.VMEM((points, width), bf16),
            pltpu.VMEM((TAPS, width, points), bf16),
            pltpu.VMEM((2, width, width), bf16),
            pltpu.VMEM((2, blocks, width, half_width), bf16),
            pltpu.SemaphoreType.DMA((2,)),
            pltpu.SemaphoreType.DMA((TAPS,)),
            pltpu.SemaphoreType.DMA((2,)),
            pltpu.SemaphoreType.DMA((2, LINE)),
        ],
        compiler_params=params(51),
        name="gradients",
    )(where, source_row, returned, slope, grad_edge, grad_node, patches)

    steps_out = (1, 2, 3)
    received = core_swap(sent)
    chip_sums = [
        (kept[i].astype(f32) + received[i].astype(f32)).astype(bf16) for i in range(len(steps_out))
    ]
    sent_own, *chip_sums = lax.optimization_barrier((sent_own, *chip_sums))
    arrived_parts = [
        lax.ppermute(chip_sum, EVERY, line_pairs(step)) for step, chip_sum in zip(steps_out, chip_sums)
    ]
    received_own = core_swap(sent_own)
    part = (chips // LINE, blocks, 16, 128)
    line_sum = pl.pallas_call(
        line_sum_kernel,
        out_shape=jax.ShapeDtypeStruct(part, bf16),
        in_specs=[whole()] * 5,
        out_specs=whole(),
        compiler_params=params(16),
        name="line_sum",
    )(kept_own, received_own, *arrived_parts)
    planes = plane_groups()
    pieces = lax.all_to_all(
        line_sum, EVERY, split_axis=0, concat_axis=0, tiled=True, axis_index_groups=planes
    )
    summed = jnp.sum(pieces.astype(f32), axis=0).astype(bf16)
    mine = lax.all_to_all(
        jnp.broadcast_to(summed[None], part), EVERY, split_axis=0, concat_axis=0, tiled=True,
        axis_index_groups=planes,
    )
    held = [lax.ppermute(mine, EVERY, line_pairs(step)) for step in steps_out]
    out_shape = (
        pltpu.HBM((TAPS, channels, width), f32),
        pltpu.HBM((1, width), f32),
        pltpu.HBM((width, width), f32),
        pltpu.HBM((width, width), f32),
    )

    def final(steps, pieces, before):
        count = len(pieces)
        return pl.pallas_call(
            functools.partial(final_kernel, steps),
            out_shape=out_shape,
            in_specs=[whole(pltpu.SMEM)] + [whole()] * count + [whole(pltpu.HBM)] * len(before),
            out_specs=(whole(pltpu.HBM),) * 4,
            scratch_shapes=[
                pltpu.VMEM((count, blocks, depth, half_width), f32),
                pltpu.VMEM((2, TAPS, channels % depth, half_width), f32),
                pltpu.VMEM((2, 1, half_width), f32),
                pltpu.SemaphoreType.DMA((count,)),
                pltpu.SemaphoreType.DMA((count, 2)),
                pltpu.SemaphoreType.DMA((count,)),
            ],
            input_output_aliases={1 + count + i: i for i in range(len(before))},
            compiler_params=params(26),
            cost_estimate=cost(0, 2 * MIB * count),
            name="final_own" if len(before) == 0 else "final_line",
        )(where, *pieces, *before)

    results = final((0,), [mine, core_swap(mine)], ())
    held[0], *results = lax.optimization_barrier((held[0], *results))
    others = [core_swap(held[0]), core_swap(held[1])]
    last, others[0] = lax.optimization_barrier((held[2], others[0]))
    others.append(core_swap(last))
    pieces = [array for pair in zip(held, others) for array in pair]
    results = final(steps_out, pieces, results)
    grad_stem, grad_bias, out_edge, out_node = results
    return (mesh_out, grad_stem, grad_bias.reshape(width), out_edge, out_node)


def solution(mesh):
    bands, columns = mesh.devices.shape
    fine = Mesh(mesh.devices.reshape(bands, columns // 2, 2), EVERY)
    in_specs = (
        P("band", ("chip", "core"), None),
        P(),
        P(),
        P(),
        P(),
        P(EVERY, None, None),
        P(EVERY, None, None),
        P(EVERY, None),
        P(EVERY, None),
    )
    out_specs = (P(EVERY, None), P(), P(), P(), P())
    return jax.shard_map(shards, mesh=fine, in_specs=in_specs, out_specs=out_specs, check_vma=False)
```

profile of v0, /device:TPU:1, one launch (start us, length us, event | category | flops | bytes accessed | tf_op | source)
XLA Modules:
  0.0 217.9 jit_solution(8370384384765351485)
XLA Ops:
  1.4 5.8 %collective-permute-start.2 = (bf16[1,1,474]{2,1,0:T(2,128)(2,1)S(1)}, bf16[1,1,474]{2,1,0:T(2,128)(2,1)S(1)}, u32[]{:S(2)}, u32[]{:S(2)}) collective-permute-start(bf16[1,1,474]{2,1,0:T(2,128)(2,1)S(1)} %slice.29), channel_id=1, source_target_pairs={{0,9},{1,10},{2,11},{3,12},{4,13},{5,14},{6,15},{7,8},{8,17},{9,18... | collective-permute-start | bytes 2852 | tf_op jit(solution)/shard_map/ppermute | solution.py:449
  8.1 3.5 %collective-permute-start.1 = (bf16[1,64,474]{2,1,0:T(8,128)(2,1)S(1)}, bf16[1,64,474]{2,1,0:T(8,128)(2,1)S(1)}, u32[]{:S(2)}, u32[]{:S(2)}) collective-permute-start(bf16[1,64,474]{2,1,0:T(8,128)(2,1)S(1)} %slice.28), channel_id=1, source_target_pairs={{0,8},{8,16},{16,24},{24,32},{32,40},{40,48},{48,56},{56,64},{64,7... | collective-permute-start | bytes 182024 | tf_op jit(solution)/shard_map/ppermute | solution.py:448
  19.6 15.5 %stem.1 = (bf16[3,32,32,512]{3,2,1,0:T(8,128)(2,1)}, bf16[3,33,32,512]{3,2,1,0:T(8,128)(2,1)}, f32[1024,512]{1,0:T(8,128)}, bf16[2048,512]{1,0:T(8,128)(2,1)}) custom-call(bf16[32,2,1,474]{3,2,1,0:T(2,128)(2,1)} %bitcast.35, bf16[1,64,474]{2,1,0:T(8,128)(2,1)} %copy-done.12, bf16[1,1,474]{2,1,0:T(2,128)(2,1)} %copy-done.14, ...), custom_call_target="tpu_custom_call" | custom-call | tf_op jit(solution)/shard_map/stem/pallas_call | solution.py:463
  35.1 8.0 %all-to-all-start = ((bf16[128,16,512]{2,1,0:T(8,128)(2,1)}), bf16[128,16,512]{2,1,0:T(8,128)(2,1)S(1)}, u32[]{:S(2)}, u32[]{:S(2)}) async-start(bf16[128,16,512]{2,1,0:T(8,128)(2,1)} %bitcast.34), calls=%async_computation | async-start | bytes 4194304 | tf_op jit(solution)/shard_map/all_to_all | solution.py:502
  47.2 26.5 %all-to-all-done = bf16[128,16,512]{2,1,0:T(8,128)(2,1)S(1)} async-done(((bf16[128,16,512]{2,1,0:T(8,128)(2,1)}), bf16[128,16,512]{2,1,0:T(8,128)(2,1)S(1)}, u32[]{:S(2)}, u32[]{:S(2)}) %all-to-all-start) | async-done | bytes 2097184 | tf_op jit(solution)/shard_map/all_to_all | solution.py:502
  75.9 5.2 %edge_back.1 = bf16[2048,512]{1,0:T(8,128)(2,1)} custom-call(bf16[512,512]{1,0:T(8,128)(2,1)S(1)} %copy-done.4, bf16[512,512]{1,0:T(8,128)(2,1)S(1)} %bitcast.31, s32[2048,1]{1,0:T(8,128)S(1)} %copy-done.2, bf16[320,512]{1,0:T(8,128)(2,1)S(1)} %convolution_convert_fusion.3.agg_ref, bf16[2048,512]{1,0:T(8,128)(2,1)S(1)} %bitcast.28), custom_call_target="tpu_custom_call" | custom-call | flops 2147483648 | bytes 8388608 | tf_op jit(solution)/shard_map/edge_back/pallas_call | solution.py:528
  81.2 5.5 %all-to-all-start.1 = ((bf16[128,16,512]{2,1,0:T(8,128)(2,1)}), bf16[128,16,512]{2,1,0:T(8,128)(2,1)}, u32[]{:S(2)}, u32[]{:S(2)}) async-start(bf16[128,16,512]{2,1,0:T(8,128)(2,1)} %bitcast.33), calls=%async_computation.1 | async-start | bytes 4194304 | tf_op jit(solution)/shard_map/all_to_all | solution.py:542
  89.9 9.7 %flip.1.patches_hbm = bf16[9,512,1024]{2,1,0:T(8,128)(2,1)} custom-call(bf16[3,32,32,512]{3,2,1,0:T(8,128)(2,1)} %get-tuple-element.44.even_ref, bf16[3,33,32,512]{3,2,1,0:T(8,128)(2,1)} %get-tuple-element.45.odd_ref), custom_call_target="tpu_custom_call" | custom-call | bytes 16777216 | tf_op jit(solution)/shard_map/flip/pallas_call | solution.py:507
  99.6 5.0 %edge_side.1 = (bf16[2048,512]{1,0:T(8,128)(2,1)}, bf16[2048,512]{1,0:T(8,128)(2,1)}) custom-call(bf16[512,512]{1,0:T(8,128)(2,1)S(1)} %copy-done.4, bf16[512,512]{1,0:T(8,128)(2,1)S(1)} %bitcast.32, s32[2048,1]{1,0:T(8,128)S(1)} %copy-done.3, bf16[320,512]{1,0:T(8,128)(2,1)S(1)} %convolution_convert_fusion.3.agg_ref, bf16[2048,512]{1,0:T(8,128)(2,1)S(1)} %bitcast.29), custom_call_target="tpu_custom_call" | custom-call | flops 2147483648 | bytes 8388608 | tf_op jit(solution)/shard_map/edge_side/pallas_call | solution.py:528
  104.6 2.5 %fusion.2 = bf16[320,512]{1,0:T(8,128)(2,1)S(1)} fusion(bf16[2048,512]{1,0:T(8,128)(2,1)} %get-tuple-element.38, s32[2048]{0:T(1024)S(1)} %eq.25), kind=kOutput, calls=%fused_computation.8 | convolution fusion | flops 671907840 | bytes 2433024 | tf_op jit(solution)/shard_map/dot_general | solution.py:19
  110.0 6.9 %all-to-all-done.1 = bf16[128,16,512]{2,1,0:T(8,128)(2,1)} async-done(((bf16[128,16,512]{2,1,0:T(8,128)(2,1)}), bf16[128,16,512]{2,1,0:T(8,128)(2,1)}, u32[]{:S(2)}, u32[]{:S(2)}) %all-to-all-start.1) | async-done | bytes 2097184 | tf_op jit(solution)/shard_map/all_to_all | solution.py:542
  116.9 12.8 %gradients.1 = (bf16[3,11,128,256]{3,2,1,0:T(8,128)(2,1)}, bf16[11,128,256]{2,1,0:T(8,128)(2,1)S(1)}, bf16[3,11,128,256]{3,2,1,0:T(8,128)(2,1)}, bf16[11,128,256]{2,1,0:T(8,128)(2,1)S(1)}) custom-call(s32[4]{0:T(128)S(1)} %broadcast_select_fusion.2.where_ref, s32[1,2048]{1,0:T(1,128)S(1)} %broadcast_select_fusion.1.source_ref, ...), custom_call_target="tpu_custom_call" | custom-call | tf_op jit(solution)/shard_map/gradients/pallas_call | solution.py:566
  131.0 4.1 %collective-permute-done.3 = bf16[3,11,128,256]{3,2,1,0:T(8,128)(2,1)S(1)} collective-permute-done((bf16[3,11,128,256]{3,2,1,0:T(8,128)(2,1)}, bf16[3,11,128,256]{3,2,1,0:T(8,128)(2,1)S(1)}, u32[]{:S(2)}, u32[]{:S(2)}) %collective-permute-start.3) | collective-permute-done | bytes 2162720 | tf_op jit(solution)/shard_map/ppermute | solution.py:35
  135.0 2.4 %fusion.5 = (bf16[11,128,256]{2,1,0:T(8,128)(2,1)S(1)}, bf16[11,128,256]{2,1,0:T(8,128)(2,1)S(1)}, bf16[11,128,256]{2,1,0:T(8,128)(2,1)S(1)}) fusion(bf16[3,11,128,256]{3,2,1,0:T(8,128)(2,1)S(1)} %collective-permute-done.3, bf16[3,11,128,256]{3,2,1,0:T(8,128)(2,1)} %get-tuple-element.48), kind=kLoop, calls=%fused_computation.13 | loop fusion | flops 4325376 | bytes 6488064 | tf_op jit(solution)/shard_map/convert_element_type | solution.py:590
  137.9 1.7 collective-permute-start.6
  140.6 16.7 %collective-permute-done.5.one_ref = bf16[11,128,256]{2,1,0:T(8,128)(2,1)S(1)} collective-permute-done((bf16[11,128,256]{2,1,0:T(8,128)(2,1)S(1)}, bf16[11,128,256]{2,1,0:T(8,128)(2,1)S(1)}, u32[]{:S(2)}, u32[]{:S(2)}) %collective-permute-start.5) | collective-permute-done | bytes 720928 | tf_op jit(solution)/shard_map/ppermute | solution.py:594
  158.3 13.8 %all_to_all.20 = bf16[16,11,16,128]{3,2,1,0:T(8,128)(2,1)S(1)} all-to-all(bf16[16,11,16,128]{3,2,1,0:T(8,128)(2,1)S(1)} %line_sum.1), channel_id=1, replica_groups={{0,8,16,24,32,40,48,56,64,72,80,88,96,104,112,120},{1,9,17,25,3,11,19,2..., dimensions={0} | all-to-all | bytes 1441792 | tf_op jit(solution)/shard_map/all_to_all | solution.py:607
  172.4 16.1 %all_to_all.21.refs_0_ = bf16[16,11,16,128]{3,2,1,0:T(8,128)(2,1)S(1)} all-to-all(bf16[16,11,16,128]{3,2,1,0:T(8,128)(2,1)S(1)} %broadcast_in_dim.36), channel_id=1, replica_groups={{0,8,16,24,32,40,48,56,64,72,80,88,96,104,112,120},{1,9,17,25,3,11,19,2..., dimensions={0} | all-to-all | bytes 1441792 | tf_op jit(solution)/shard_map/all_to_all | solution.py:611
  188.5 1.9 collective-permute-start.9
  191.2 2.5 %collective-permute-start.12 = (bf16[16,11,16,128]{3,2,1,0:T(8,128)(2,1)S(1)}, bf16[16,11,16,128]{3,2,1,0:T(8,128)(2,1)S(1)}, u32[]{:S(2)}, u32[]{:S(2)}) collective-permute-start(bf16[16,11,16,128]{3,2,1,0:T(8,128)(2,1)S(1)} %all_to_all.21.refs_0_), channel_id=1, source_target_pairs={{0,4},{1,65},{2,6},{3,67},{4,0},{5,69},{6,2},{7,71},{8,12},{9,73},... | collective-permute-start | bytes 2162696 | tf_op jit(solution)/shard_map/ppermute | solution.py:615
  193.8 2.3 %final_own.1 = (f32[9,474,512]{2,1,0:T(8,128)}, f32[1,512]{1,0:T(1,128)}, f32[512,512]{1,0:T(8,128)}, f32[512,512]{1,0:T(8,128)}) custom-call(s32[4]{0:T(128)S(1)} %broadcast_select_fusion.2.where_ref, bf16[16,11,16,128]{3,2,1,0:T(8,128)(2,1)S(1)} %all_to_all.21.refs_0_, bf16[16,11,16,128]{3,2,1,0:T(8,128)(2,1)S(1)} %collective-permute-done.9.refs_1_), custom_call_target="tpu_custom_call" | custom-call | bytes 4194304 | tf_op jit(solution)/shard_map/final_own/pallas_call | solution.py:625
  196.1 5.9 %collective-permute-done.8.refs_0_ = bf16[16,11,16,128]{3,2,1,0:T(8,128)(2,1)S(1)} collective-permute-done((bf16[16,11,16,128]{3,2,1,0:T(8,128)(2,1)S(1)}, bf16[16,11,16,128]{3,2,1,0:T(8,128)(2,1)S(1)}, u32[]{:S(2)}, u32[]{:S(2)}) %collective-permute-start.8) | collective-permute-done | bytes 720928 | tf_op jit(solution)/shard_map/ppermute | solution.py:615
  202.9 7.5 %collective-permute-done.12.refs_2_ = bf16[16,11,16,128]{3,2,1,0:T(8,128)(2,1)S(1)} collective-permute-done((bf16[16,11,16,128]{3,2,1,0:T(8,128)(2,1)S(1)}, bf16[16,11,16,128]{3,2,1,0:T(8,128)(2,1)S(1)}, u32[]{:S(2)}, u32[]{:S(2)}) %collective-permute-start.12) | collective-permute-done | bytes 720928 | tf_op jit(solution)/shard_map/ppermute | solution.py:615
  213.6 4.1 %final_line.1 = (f32[9,474,512]{2,1,0:T(8,128)}, f32[1,512]{1,0:T(1,128)}, f32[512,512]{1,0:T(8,128)}, f32[512,512]{1,0:T(8,128)}) custom-call(s32[4]{0:T(128)S(1)} %broadcast_select_fusion.2.where_ref, bf16[16,11,16,128]{3,2,1,0:T(8,128)(2,1)S(1)} %collective-permute-done.8.refs_0_, ...), custom_call_target="tpu_custom_call", output_to_operand_aliasing={{0}: (7, {}), {1}: (8, {}), {2}: (9, {}), {3}: (10, {})} | custom-call | bytes 12582912 | tf_op jit(solution)/shard_map/final_line/pallas_call | solution.py:625
  (80 shorter events, 30.8 us)
Async XLA Ops:
  0.6 45.2 %copy-start = (bf16[512,512]{1,0:T(8,128)(2,1)S(1)}, bf16[512,512]{1,0:T(8,128)(2,1)}, u32[]{:S(2)}) copy-start(bf16[512,512]{1,0:T(8,128)(2,1)} %param.13) | copy-start | bytes 1572868
  1.4 17.5 %collective-permute-start.2 = (bf16[1,1,474]{2,1,0:T(2,128)(2,1)S(1)}, bf16[1,1,474]{2,1,0:T(2,128)(2,1)S(1)}, u32[]{:S(2)}, u32[]{:S(2)}) collective-permute-start(bf16[1,1,474]{2,1,0:T(2,128)(2,1)S(1)} %slice.29), channel_id=1, source_target_pairs={{0,9},{1,10},{2,11},{3,12},{4,13},{5,14},{6,15},{7,8},{8,17},{9,18... | collective-permute-start | bytes 2852 | tf_op jit(solution)/shard_map/ppermute | solution.py:449
  8.1 10.8 %collective-permute-start.1 = (bf16[1,64,474]{2,1,0:T(8,128)(2,1)S(1)}, bf16[1,64,474]{2,1,0:T(8,128)(2,1)S(1)}, u32[]{:S(2)}, u32[]{:S(2)}) collective-permute-start(bf16[1,64,474]{2,1,0:T(8,128)(2,1)S(1)} %slice.28), channel_id=1, source_target_pairs={{0,8},{8,16},{16,24},{24,32},{32,40},{40,48},{48,56},{56,64},{64,7... | collective-permute-start | bytes 182024 | tf_op jit(solution)/shard_map/ppermute | solution.py:448
  12.8 6.1 %collective-permute-start = (bf16[64,1,474]{2,1,0:T(2,128)(2,1)S(1)}, bf16[64,1,474]{2,1,0:T(2,128)(2,1)S(1)}, u32[]{:S(2)}, u32[]{:S(2)}) collective-permute-start(bf16[64,1,474]{2,1,0:T(2,128)(2,1)S(1)} %slice.27), channel_id=1, source_target_pairs={{0,1},{1,2},{2,3},{3,4},{4,5},{5,6},{6,7},{7,0},{8,9},{9,10},{10,1... | collective-permute-start | bytes 182024 | tf_op jit(solution)/shard_map/ppermute | solution.py:445
  35.1 8.1 %copy-start.13 = (s32[1,128,16]{1,2,0:T(8,128)S(1)}, s32[1,128,16]{1,2,0:T(8,128)}, u32[]{:S(2)}) copy-start(s32[1,128,16]{1,2,0:T(8,128)} %param.15) | copy-start | bytes 24580
  35.1 8.2 %copy-start.4 = (bf16[512,512]{1,0:T(8,128)(2,1)S(1)}, bf16[512,512]{1,0:T(8,128)(2,1)}, u32[]{:S(2)}) copy-start(bf16[512,512]{1,0:T(8,128)(2,1)} %w_ref.3) | copy-start | bytes 1572868
  35.1 38.5 %all-to-all-start = ((bf16[128,16,512]{2,1,0:T(8,128)(2,1)}), bf16[128,16,512]{2,1,0:T(8,128)(2,1)S(1)}, u32[]{:S(2)}, u32[]{:S(2)}) async-start(bf16[128,16,512]{2,1,0:T(8,128)(2,1)} %bitcast.34), calls=%async_computation | async-start | bytes 4194304 | tf_op jit(solution)/shard_map/all_to_all | solution.py:502
  81.2 35.8 %all-to-all-start.1 = ((bf16[128,16,512]{2,1,0:T(8,128)(2,1)}), bf16[128,16,512]{2,1,0:T(8,128)(2,1)}, u32[]{:S(2)}, u32[]{:S(2)}) async-start(bf16[128,16,512]{2,1,0:T(8,128)(2,1)} %bitcast.33), calls=%async_computation.1 | async-start | bytes 4194304 | tf_op jit(solution)/shard_map/all_to_all | solution.py:542
  89.9 9.7 %copy-start.3 = (s32[2048,1]{1,0:T(8,128)S(1)}, s32[2048,1]{1,0:T(8,128)}, u32[]{:S(2)}) copy-start(s32[2048,1]{1,0:T(8,128)} %reshape_reshape.4.dst_ref) | copy-start | bytes 24580
  89.9 9.7 %copy-start.6 = (bf16[512,512]{0,1:T(8,128)(2,1)S(1)}, bf16[512,512]{0,1:T(8,128)(2,1)}, u32[]{:S(2)}) copy-start(bf16[512,512]{0,1:T(8,128)(2,1)} %copy.23) | copy-start | bytes 1572868
  104.6 3.6 %copy-start.9 = (bf16[320,512]{1,0:T(8,128)(2,1)S(1)}, bf16[320,512]{1,0:T(8,128)(2,1)}, u32[]{:S(2)}) copy-start(bf16[320,512]{1,0:T(8,128)(2,1)} %param.17) | copy-start | bytes 983044
  129.8 5.3 %collective-permute-start.3 = (bf16[3,11,128,256]{3,2,1,0:T(8,128)(2,1)}, bf16[3,11,128,256]{3,2,1,0:T(8,128)(2,1)S(1)}, u32[]{:S(2)}, u32[]{:S(2)}) collective-permute-start(bf16[3,11,128,256]{3,2,1,0:T(8,128)(2,1)} %get-tuple-element.49), channel_id=1, source_target_pairs={{0,1},{1,0},{2,3},{3,2},{4,5},{5,4},{6,7},{7,6},{8,9},{9,8},{10,11... | collective-permute-start | bytes 6488072 | tf_op jit(solution)/shard_map/ppermute | solution.py:35
  137.5 3.1 %collective-permute-start.4 = (bf16[11,128,256]{2,1,0:T(8,128)(2,1)S(1)}, bf16[11,128,256]{2,1,0:T(8,128)(2,1)S(1)}, u32[]{:S(2)}, u32[]{:S(2)}) collective-permute-start(bf16[11,128,256]{2,1,0:T(8,128)(2,1)S(1)} %get-tuple-element.50), channel_id=1, source_target_pairs={{0,1},{1,0},{2,3},{3,2},{4,5},{5,4},{6,7},{7,6},{8,9},{9,8},{10,11... | collective-permute-start | bytes 2162696 | tf_op jit(solution)/shard_map/ppermute | solution.py:35
  137.9 19.4 %collective-permute-start.5 = (bf16[11,128,256]{2,1,0:T(8,128)(2,1)S(1)}, bf16[11,128,256]{2,1,0:T(8,128)(2,1)S(1)}, u32[]{:S(2)}, u32[]{:S(2)}) collective-permute-start(bf16[11,128,256]{2,1,0:T(8,128)(2,1)S(1)} %get-tuple-element.51), channel_id=1, source_target_pairs={{0,2},{1,33},{2,4},{3,35},{4,6},{5,37},{6,0},{7,39},{8,10},{9,41},... | collective-permute-start | bytes 2162696 | tf_op jit(solution)/shard_map/ppermute | solution.py:594
  137.9 19.4 %collective-permute-start.6 = (bf16[11,128,256]{2,1,0:T(8,128)(2,1)S(1)}, bf16[11,128,256]{2,1,0:T(8,128)(2,1)S(1)}, u32[]{:S(2)}, u32[]{:S(2)}) collective-permute-start(bf16[11,128,256]{2,1,0:T(8,128)(2,1)S(1)} %get-tuple-element.52), channel_id=1, source_target_pairs={{0,4},{1,65},{2,6},{3,67},{4,0},{5,69},{6,2},{7,71},{8,12},{9,73},... | collective-permute-start | bytes 2162696 | tf_op jit(solution)/shard_map/ppermute | solution.py:594
  139.6 18.3 %collective-permute-start.7 = (bf16[11,128,256]{2,1,0:T(8,128)(2,1)S(1)}, bf16[11,128,256]{2,1,0:T(8,128)(2,1)S(1)}, u32[]{:S(2)}, u32[]{:S(2)}) collective-permute-start(bf16[11,128,256]{2,1,0:T(8,128)(2,1)S(1)} %get-tuple-element.53), channel_id=1, source_target_pairs={{0,6},{1,97},{2,0},{3,99},{4,2},{5,101},{6,4},{7,103},{8,14},{9,10... | collective-permute-start | bytes 2162696 | tf_op jit(solution)/shard_map/ppermute | solution.py:594
  188.5 5.4 %collective-permute-start.9 = (bf16[16,11,16,128]{3,2,1,0:T(8,128)(2,1)S(1)}, bf16[16,11,16,128]{3,2,1,0:T(8,128)(2,1)S(1)}, u32[]{:S(2)}, u32[]{:S(2)}) collective-permute-start(bf16[16,11,16,128]{3,2,1,0:T(8,128)(2,1)S(1)} %all_to_all.21.refs_0_), channel_id=1, source_target_pairs={{0,1},{1,0},{2,3},{3,2},{4,5},{5,4},{6,7},{7,6},{8,9},{9,8},{10,11... | collective-permute-start | bytes 2162696 | tf_op jit(solution)/shard_map/ppermute | solution.py:35
  190.4 11.6 %collective-permute-start.8 = (bf16[16,11,16,128]{3,2,1,0:T(8,128)(2,1)S(1)}, bf16[16,11,16,128]{3,2,1,0:T(8,128)(2,1)S(1)}, u32[]{:S(2)}, u32[]{:S(2)}) collective-permute-start(bf16[16,11,16,128]{3,2,1,0:T(8,128)(2,1)S(1)} %all_to_all.21.refs_0_), channel_id=1, source_target_pairs={{0,2},{1,33},{2,4},{3,35},{4,6},{5,37},{6,0},{7,39},{8,10},{9,41},... | collective-permute-start | bytes 2162696 | tf_op jit(solution)/shard_map/ppermute | solution.py:615
  191.2 19.1 %collective-permute-start.12 = (bf16[16,11,16,128]{3,2,1,0:T(8,128)(2,1)S(1)}, bf16[16,11,16,128]{3,2,1,0:T(8,128)(2,1)S(1)}, u32[]{:S(2)}, u32[]{:S(2)}) collective-permute-start(bf16[16,11,16,128]{3,2,1,0:T(8,128)(2,1)S(1)} %all_to_all.21.refs_0_), channel_id=1, source_target_pairs={{0,4},{1,65},{2,6},{3,67},{4,0},{5,69},{6,2},{7,71},{8,12},{9,73},... | collective-permute-start | bytes 2162696 | tf_op jit(solution)/shard_map/ppermute | solution.py:615
  193.8 17.0 %collective-permute-start.10 = (bf16[16,11,16,128]{3,2,1,0:T(8,128)(2,1)S(1)}, bf16[16,11,16,128]{3,2,1,0:T(8,128)(2,1)S(1)}, u32[]{:S(2)}, u32[]{:S(2)}) collective-permute-start(bf16[16,11,16,128]{3,2,1,0:T(8,128)(2,1)S(1)} %all_to_all.21.refs_0_), channel_id=1, source_target_pairs={{0,6},{1,97},{2,0},{3,99},{4,2},{5,101},{6,4},{7,103},{8,14},{9,10... | collective-permute-start | bytes 2162696 | tf_op jit(solution)/shard_map/ppermute | solution.py:615
  202.0 8.8 %collective-permute-start.11 = (bf16[16,11,16,128]{3,2,1,0:T(8,128)(2,1)S(1)}, bf16[16,11,16,128]{3,2,1,0:T(8,128)(2,1)S(1)}, u32[]{:S(2)}, u32[]{:S(2)}) collective-permute-start(bf16[16,11,16,128]{3,2,1,0:T(8,128)(2,1)S(1)} %collective-permute-done.8.refs_0_), channel_id=1, source_target_pairs={{0,1},{1,0},{2,3},{3,2},{4,5},{5,4},{6,7},{7,6},{8,9},{9,8},{10,11... | collective-permute-start | bytes 2162696 | tf_op jit(solution)/shard_map/ppermute | solution.py:35
  210.4 2.2 %collective-permute-start.13 = (bf16[16,11,16,128]{3,2,1,0:T(8,128)(2,1)S(1)}, bf16[16,11,16,128]{3,2,1,0:T(8,128)(2,1)S(1)}, u32[]{:S(2)}, u32[]{:S(2)}) collective-permute-start(bf16[16,11,16,128]{3,2,1,0:T(8,128)(2,1)S(1)} %collective-permute-done.12.refs_2_), channel_id=1, source_target_pairs={{0,1},{1,0},{2,3},{3,2},{4,5},{5,4},{6,7},{7,6},{8,9},{9,8},{10,11... | collective-permute-start | bytes 2162696 | tf_op jit(solution)/shard_map/ppermute | solution.py:35
  210.8 2.8 %collective-permute-start.14 = (bf16[16,11,16,128]{3,2,1,0:T(8,128)(2,1)S(1)}, bf16[16,11,16,128]{3,2,1,0:T(8,128)(2,1)S(1)}, u32[]{:S(2)}, u32[]{:S(2)}) collective-permute-start(bf16[16,11,16,128]{3,2,1,0:T(8,128)(2,1)S(1)} %collective-permute-done.10.refs_4_), channel_id=1, source_target_pairs={{0,1},{1,0},{2,3},{3,2},{4,5},{5,4},{6,7},{7,6},{8,9},{9,8},{10,11... | collective-permute-start | bytes 2162696 | tf_op jit(solution)/shard_map/ppermute | solution.py:35
  213.6 4.1 %copy-start.1 = (bf16[512,512]{1,0:T(8,128)(2,1)S(1)}, bf16[512,512]{1,0:T(8,128)(2,1)}, u32[]{:S(2)}) copy-start(bf16[512,512]{1,0:T(8,128)(2,1)} %param.13) | copy-start | bytes 1572868
  (8 other events, 7.7 us)
where the time goes:
time: 219 us; the launch traced here: 218 us
  waiting for transfers between devices  70.3 us (32%)
  Pallas kernels  55 us (25%)
  starting transfers between devices  34.8 us (16%)
  blocking collectives  29.9 us (14%)
  local copies, waits for them, and re-layouts  13.1 us (6%)
  other arithmetic  7.02 us (3%)
  matrix products  6.62 us (3%)
    all_to_all x1, waiting for transfers between devices, shards(): lax.all_to_all(outgoing.reshape(device_count, slot_count, width), EVERY,...  26.5 us
    ppermute x3, waiting for transfers between devices, shards(): lax.ppermute(chip_sum, EVERY, line_pairs(step))  17.3 us
    all_to_all x1, blocking collectives, shards(): lax.all_to_all(jnp.broadcast_to(summed[None], part), EVERY, split_axis=0,...  16.1 us
    pallas_call x1, Pallas kernels, shards(): pl.pallas_call(stem_kernel, out_shape=(pltpu.HBM((3, half_rows, half_cols...  15.5 us
    all_to_all x1, blocking collectives, shards(): lax.all_to_all(line_sum, EVERY, split_axis=0, concat_axis=0, tiled=True,...  13.8 us
    ppermute x3, waiting for transfers between devices, shards(): held = [lax.ppermute(mine, EVERY, line_pairs(step)) for step in steps_out]  13.4 us
    pallas_call x1, Pallas kernels, shards(): pl.pallas_call(gradients_kernel, out_shape=(line_shape, own_shape) * 2, i...  12.8 us
    pallas_call x2, Pallas kernels, edge_call(): pl.pallas_call(functools.partial(edge_kernel, side), out_shape=(pltpu.HBM...  10.2 us
  transfers between devices with their start and end apart: 17, of which 9 were waited for; matrix products, arithmetic and copies ran while one was open for 9% of the time, Pallas kernels for 8%

commit v1 on v0

--- a/solution.py
+++ b/solution.py
@@ -3,6 +3,7 @@
 
 import jax
 import jax.numpy as jnp
+import numpy as np
 from jax import lax
 from jax.experimental import pallas as pl
 from jax.experimental.pallas import tpu as pltpu
@@ -11,8 +12,9 @@
 EVERY = ("band", "chip", "core")
 TAPS = 9
 LINE = 4
+ORDER = (2, 1, 3, 0)
 MIB = 1024 * 1024
-TILE = 256
+TILE = 512
 
 
 def f32_dot(first, second):
@@ -76,22 +78,14 @@
     return pl.loop(0, count, unroll=True)
 
 
-def column_picker(image_rows, cols, parts):
+def column_picker(image_rows, cols):
     half = cols // 2
-    shape = (3 * image_rows * half, image_rows * cols)
-    out = lax.broadcasted_iota(jnp.int32, shape, 0)
-    inside = lax.broadcasted_iota(jnp.int32, shape, 1)
-    per_tap = image_rows * half
-    tap = out // per_tap
-    rest = out - tap * per_tap
-    line = rest // half
-    col = 2 * (rest - line * half) + tap - 1
-    if parts == 2:
-        pairs = image_rows // 2
-        parity = line // pairs
-        line = 2 * (line - parity * pairs) + parity
-    hit = (col >= 0) & (inside == line * cols + col)
-    return jnp.where(hit, 1.0, 0.0).astype(jnp.bfloat16)
+    out = np.zeros((3, image_rows, half, image_rows, cols), np.float32)
+    lines = [*range(0, image_rows, 2), *range(1, image_rows, 2)]
+    for tap, (place, line), j in itertools.product(range(3), enumerate(lines), range(half)):
+        if 2 * j + tap >= 1:
+            out[tap, place, j, line, 2 * j + tap - 1] = 1.0
+    return jnp.asarray(out.reshape(3 * image_rows * half, image_rows * cols), jnp.bfloat16)
 
 
 def stem_kernel(
@@ -254,9 +248,9 @@
     @unrolled(tiles)
     def _(step):
         here = rows_at(step, tile)
-        node = lax.broadcasted_iota(jnp.int32, (tile, nodes), 1)
-        pick = jnp.where(node == dst_ref[here], 1.0, 0.0).astype(bf16)
-        grad_msg = f32_dot(pick, agg_ref[...])
+        node = lax.broadcasted_iota(jnp.int32, (nodes, tile), 0)
+        pick = jnp.where(node == dst_ref[:, here], 1.0, 0.0).astype(bf16)
+        grad_msg = inner_dot(pick, agg_ref[...])
         load(step).wait()
 
         @pl.when(step + 1 < tiles)
@@ -285,9 +279,12 @@
 
 def gradients_kernel(
     where_ref, source_ref, returned_hbm, slope_hbm, edge_hbm, node_hbm, patches_hbm,
-    sent_line_hbm, sent_own_hbm, kept_line_hbm, kept_own_hbm,
-    returned, slope, stemout, patches, smalls, out, before_sems, patch_sems, small_sems, out_sems,
+    *refs,
 ):
+    placed = (refs[:LINE], refs[LINE : 2 * LINE])
+    (
+        returned, slope, stemout, patches, smalls, out, before_sems, patch_sems, small_sems, out_sems,
+    ) = refs[2 * LINE :]
     half_width = out.shape[3]
     depth = out.shape[2] // LINE
     points, width = stemout.shape
@@ -305,15 +302,13 @@
         pltpu.make_async_copy(placed, smalls.at[number], small_sems.at[number])
         for number, placed in enumerate((edge_hbm, node_hbm))
     ]
-    placed = ((sent_line_hbm, sent_own_hbm), (kept_line_hbm, kept_own_hbm))
 
     def stores(part):
         copies = []
         for slot in range(LINE):
-            quarter = quarter_of(where_ref[3 - part], slot + 1)
-            target = placed[part][0].at[slot] if slot < LINE - 1 else placed[part][1]
+            quarter = quarter_of(where_ref[3 - part], ORDER[slot])
             copies.append(
-                pltpu.make_async_copy(out.at[part, :, pl.ds(pl.multiple_of(quarter * depth, depth), depth)], target, out_sems.at[part, slot])
+                pltpu.make_async_copy(out.at[part, :, pl.ds(pl.multiple_of(quarter * depth, depth), depth)], placed[part][slot], out_sems.at[part, slot])
             )
         return copies
 
@@ -491,8 +486,8 @@
         west.reshape(half_rows, 2, 1, channels),
         north,
         corner,
-        column_picker(4, cols_here, 2),
-        column_picker(1, cols_here, 1),
+        column_picker(4, cols_here),
+        column_picker(1, cols_here),
         b_stem.reshape(1, width),
         source.reshape(slots, 1),
         grid_input,
@@ -520,7 +515,7 @@
     grad_agg = right_dot(mesh_cotangent, w_node).astype(bf16)
     dst_flat = dst_index.reshape(slots)
 
-    dst_column = dst_flat.reshape(slots, 1)
+    dst_row = dst_flat.reshape(1, slots)
     w_flipped = w_edge.T
 
     def edge_call(side):
@@ -535,7 +530,7 @@
             compiler_params=params(40),
             cost_estimate=cost(4 * slots * width * width, 8 * MIB),
             name="edge_side" if side else "edge_back",
-        )(w_edge, w_flipped, dst_column, grad_agg, arrived)
+        )(w_edge, w_flipped, dst_row, grad_agg, arrived)
 
     (back,) = edge_call(False)
 
@@ -561,13 +556,11 @@
     depth = width // LINE
     source_row = source.reshape(1, slots)
     quarter_shape = (blocks, depth, half_width)
-    line_shape = jax.ShapeDtypeStruct((LINE - 1,) + quarter_shape, bf16)
-    own_shape = jax.ShapeDtypeStruct(quarter_shape, bf16)
-    sent, sent_own, kept, kept_own = pl.pallas_call(
+    quarters = pl.pallas_call(
         gradients_kernel,
-        out_shape=(line_shape, own_shape) * 2,
+        out_shape=(jax.ShapeDtypeStruct(quarter_shape, bf16),) * (2 * LINE),
         in_specs=[whole(pltpu.SMEM), whole()] + [whole(pltpu.HBM)] * 5,
-        out_specs=(whole(pl.ANY),) * 4,
+        out_specs=(whole(pl.ANY),) * (2 * LINE),
         scratch_shapes=[
             pltpu.VMEM((slots, width), bf16),
             pltpu.VMEM((points, width), f32),
@@ -584,15 +577,16 @@
         name="gradients",
     )(where, source_row, returned, slope, grad_edge, grad_node, patches)
 
-    steps_out = (1, 2, 3)
-    received = core_swap(sent)
+    sent, kept = quarters[:LINE], quarters[LINE:]
+    steps_out = ORDER[:-1]
+    received = [core_swap(array) for array in sent[:-1]]
     chip_sums = [
-        (kept[i].astype(f32) + received[i].astype(f32)).astype(bf16) for i in range(len(steps_out))
-    ]
-    sent_own, *chip_sums = lax.optimization_barrier((sent_own, *chip_sums))
+        (one.astype(f32) + other.astype(f32)).astype(bf16) for one, other in zip(kept, received)
+    ]
     arrived_parts = [
         lax.ppermute(chip_sum, EVERY, line_pairs(step)) for step, chip_sum in zip(steps_out, chip_sums)
     ]
+    sent_own, chip_sums[-1] = lax.optimization_barrier((sent[-1], chip_sums[-1]))
     received_own = core_swap(sent_own)
     part = (chips // LINE, blocks, 16, 128)
     line_sum = pl.pallas_call(
@@ -602,7 +596,7 @@
         out_specs=whole(),
         compiler_params=params(16),
         name="line_sum",
-    )(kept_own, received_own, *arrived_parts)
+    )(kept[-1], received_own, *arrived_parts)
     planes = plane_groups()
     pieces = lax.all_to_all(
         line_sum, EVERY, split_axis=0, concat_axis=0, tiled=True, axis_index_groups=planes

time: 219 us -> 212 us (0.968)
  other arithmetic: 7.02 us -> 4.45 us
  waiting for transfers between devices: 70.3 us -> 68 us
    convert_element_type x3, other arithmetic: 4.28 us -> 1.72 us  [shards(): (one.astype(f32) + other.astype(f32)).astype(bf16)]
    ppermute x6 -> x8, waiting for transfers between devices: 6.21 us -> 4.39 us  [core_swap(): return lax.ppermute(array, 'core', [(0, 1), (1, 0)])]
    unnamed x33 -> x37, local copies, waits for them, and re-layouts: 5.04 us -> 4.36 us
    ppermute x6 -> x8, starting transfers between devices: 5.55 us -> 5.67 us  [core_swap(): return lax.ppermute(array, 'core', [(0, 1), (1, 0)])]
  transfers between devices with their start and end apart: 17 -> 19, of which waited for: 9 -> 10; matrix products, arithmetic and copies ran while one was open for 9% -> 9% of each run, Pallas kernels for 8% -> 8%
where the time goes in v1:
time: 212 us
  waiting for transfers between devices  68 us (32%)
  Pallas kernels  54.3 us (26%)
  starting transfers between devices  35.5 us (17%)
  blocking collectives  30 us (14%)
  local copies, waits for them, and re-layouts  11.6 us (5%)
  matrix products  6.62 us (3%)
  other arithmetic  4.45 us (2%)
    all_to_all x1, waiting for transfers between devices, shards(): lax.all_to_all(outgoing.reshape(device_count, slot_count, width), EVERY,...  27.4 us
    ppermute x3, waiting for transfers between devices, shards(): lax.ppermute(chip_sum, EVERY, line_pairs(step))  18 us
    all_to_all x1, blocking collectives, shards(): lax.all_to_all(jnp.broadcast_to(summed[None], part), EVERY, split_axis=0,...  16.3 us
    pallas_call x1, Pallas kernels, shards(): pl.pallas_call(stem_kernel, out_shape=(pltpu.HBM((3, half_rows, half_cols...  14.5 us
    all_to_all x1, blocking collectives, shards(): lax.all_to_all(line_sum, EVERY, split_axis=0, concat_axis=0, tiled=True,...  13.7 us
    pallas_call x1, Pallas kernels, shards(): pl.pallas_call(gradients_kernel, out_shape=(jax.ShapeDtypeStruct(quarter_...  13.1 us
    ppermute x3, waiting for transfers between devices, shards(): held = [lax.ppermute(mine, EVERY, line_pairs(step)) for step in steps_out]  12 us
    pallas_call x2, Pallas kernels, edge_call(): pl.pallas_call(functools.partial(edge_kernel, side), out_shape=(pltpu.HBM...  10.3 us
  transfers between devices with their start and end apart: 19, of which 10 were waited for; matrix products, arithmetic and copies ran while one was open for 9% of the time, Pallas kernels for 8%

profile of v1, /device:TPU:1, one launch (start us, length us, event | category | flops | bytes accessed | tf_op | source)
XLA Modules:
  0.0 211.5 jit_solution(9683668314142513291)
XLA Ops:
  1.4 5.8 %collective-permute-start.2 = (bf16[1,1,474]{2,1,0:T(2,128)(2,1)S(1)}, bf16[1,1,474]{2,1,0:T(2,128)(2,1)S(1)}, u32[]{:S(2)}, u32[]{:S(2)}) collective-permute-start(bf16[1,1,474]{2,1,0:T(2,128)(2,1)S(1)} %slice.11), channel_id=1, source_target_pairs={{0,9},{1,10},{2,11},{3,12},{4,13},{5,14},{6,15},{7,8},{8,17},{9,18... | collective-permute-start | bytes 2852 | tf_op jit(solution)/shard_map/ppermute | solution.py:444
  8.1 3.5 %collective-permute-start.1 = (bf16[1,64,474]{2,1,0:T(8,128)(2,1)S(1)}, bf16[1,64,474]{2,1,0:T(8,128)(2,1)S(1)}, u32[]{:S(2)}, u32[]{:S(2)}) collective-permute-start(bf16[1,64,474]{2,1,0:T(8,128)(2,1)S(1)} %slice.10), channel_id=1, source_target_pairs={{0,8},{8,16},{16,24},{24,32},{32,40},{40,48},{48,56},{56,64},{64,7... | collective-permute-start | bytes 182024 | tf_op jit(solution)/shard_map/ppermute | solution.py:443
  17.7 14.5 %stem.1 = (bf16[3,32,32,512]{3,2,1,0:T(8,128)(2,1)}, bf16[3,33,32,512]{3,2,1,0:T(8,128)(2,1)}, f32[1024,512]{1,0:T(8,128)}, bf16[2048,512]{1,0:T(8,128)(2,1)}) custom-call(bf16[32,2,1,474]{3,2,1,0:T(2,128)(2,1)} %bitcast.29, bf16[1,64,474]{2,1,0:T(8,128)(2,1)} %copy-done.13, bf16[1,1,474]{2,1,0:T(2,128)(2,1)} %copy-done.15, ...), custom_call_target="tpu_custom_call" | custom-call | tf_op jit(solution)/shard_map/stem/pallas_call | solution.py:458
  32.2 8.0 %all-to-all-start = ((bf16[128,16,512]{2,1,0:T(8,128)(2,1)}), bf16[128,16,512]{2,1,0:T(8,128)(2,1)S(1)}, u32[]{:S(2)}, u32[]{:S(2)}) async-start(bf16[128,16,512]{2,1,0:T(8,128)(2,1)} %bitcast.28), calls=%async_computation | async-start | bytes 4194304 | tf_op jit(solution)/shard_map/all_to_all | solution.py:497
  43.3 27.4 %all-to-all-done = bf16[128,16,512]{2,1,0:T(8,128)(2,1)S(1)} async-done(((bf16[128,16,512]{2,1,0:T(8,128)(2,1)}), bf16[128,16,512]{2,1,0:T(8,128)(2,1)S(1)}, u32[]{:S(2)}, u32[]{:S(2)}) %all-to-all-start) | async-done | bytes 2097184 | tf_op jit(solution)/shard_map/all_to_all | solution.py:497
  71.8 5.2 %edge_back.1 = bf16[2048,512]{1,0:T(8,128)(2,1)} custom-call(bf16[512,512]{1,0:T(8,128)(2,1)S(1)} %copy-done.3, bf16[512,512]{1,0:T(8,128)(2,1)S(1)} %bitcast.25, s32[1,2048]{1,0:T(1,128)S(1)} %broadcast_in_dim_reshape.3.dst_ref, bf16[320,512]{1,0:T(8,128)(2,1)S(1)} %convolution_convert_fusion.3.agg_ref, bf16[2048,512]{1,0:T(8,128)(2,1)S(1)} %bitcast.22), custom_call_target="tpu_custom_call" | custom-call | flops 2147483648 | bytes 8388608 | tf_op jit(solution)/shard_map/edge_back/pallas_call | solution.py:523
  77.0 5.5 %all-to-all-start.1 = ((bf16[128,16,512]{2,1,0:T(8,128)(2,1)}), bf16[128,16,512]{2,1,0:T(8,128)(2,1)}, u32[]{:S(2)}, u32[]{:S(2)}) async-start(bf16[128,16,512]{2,1,0:T(8,128)(2,1)} %bitcast.27), calls=%async_computation.1 | async-start | bytes 4194304 | tf_op jit(solution)/shard_map/all_to_all | solution.py:537
  86.3 9.6 %flip.1.patches_hbm = bf16[9,512,1024]{2,1,0:T(8,128)(2,1)} custom-call(bf16[3,32,32,512]{3,2,1,0:T(8,128)(2,1)} %get-tuple-element.45.even_ref, bf16[3,33,32,512]{3,2,1,0:T(8,128)(2,1)} %get-tuple-element.46.odd_ref), custom_call_target="tpu_custom_call" | custom-call | bytes 16777216 | tf_op jit(solution)/shard_map/flip/pallas_call | solution.py:502
  95.9 5.1 %edge_side.1 = (bf16[2048,512]{1,0:T(8,128)(2,1)}, bf16[2048,512]{1,0:T(8,128)(2,1)}) custom-call(bf16[512,512]{1,0:T(8,128)(2,1)S(1)} %copy-done.3, bf16[512,512]{1,0:T(8,128)(2,1)S(1)} %bitcast.26, s32[1,2048]{1,0:T(1,128)S(1)} %broadcast_in_dim_reshape.3.dst_ref, bf16[320,512]{1,0:T(8,128)(2,1)S(1)} %convolution_convert_fusion.3.agg_ref, ...), custom_call_target="tpu_custom_call" | custom-call | flops 2147483648 | bytes 8388608 | tf_op jit(solution)/shard_map/edge_side/pallas_call | solution.py:523
  101.1 2.5 %fusion.2 = bf16[320,512]{1,0:T(8,128)(2,1)S(1)} fusion(bf16[2048,512]{1,0:T(8,128)(2,1)} %get-tuple-element.39, s32[2048]{0:T(1024)S(1)} %eq.19), kind=kOutput, calls=%fused_computation.8 | convolution fusion | flops 671907840 | bytes 2433024 | tf_op jit(solution)/shard_map/dot_general | solution.py:21
  106.6 6.2 %all-to-all-done.1 = bf16[128,16,512]{2,1,0:T(8,128)(2,1)} async-done(((bf16[128,16,512]{2,1,0:T(8,128)(2,1)}), bf16[128,16,512]{2,1,0:T(8,128)(2,1)}, u32[]{:S(2)}, u32[]{:S(2)}) %all-to-all-start.1) | async-done | bytes 2097184 | tf_op jit(solution)/shard_map/all_to_all | solution.py:537
  112.7 13.1 %gradients.1 = (bf16[11,128,256]{2,1,0:T(8,128)(2,1)S(1)}, bf16[11,128,256]{2,1,0:T(8,128)(2,1)S(1)}, bf16[11,128,256]{2,1,0:T(8,128)(2,1)}, bf16[11,128,256]{2,...) custom-call(s32[4]{0:T(128)S(1)} %broadcast_select_fusion.2.where_re, ...), custom_call_target="tpu_custom_call" | custom-call | tf_op jit(solution)/shard_map/gradients/pallas_call | solution.py:559
  133.6 7.5 %collective-permute-done.9.three_ref = bf16[11,128,256]{2,1,0:T(8,128)(2,1)S(1)} collective-permute-done((bf16[11,128,256]{2,1,0:T(8,128)(2,1)S(1)}, bf16[11,128,256]{2,1,0:T(8,128)(2,1)S(1)}, u32[]{:S(2)}, u32[]{:S(2)}) %collective-permute-start.9) | collective-permute-done | bytes 720928 | tf_op jit(solution)/shard_map/ppermute | solution.py:587
  141.1 2.8 %collective-permute-done.6.one_ref = bf16[11,128,256]{2,1,0:T(8,128)(2,1)S(1)} collective-permute-done((bf16[11,128,256]{2,1,0:T(8,128)(2,1)S(1)}, bf16[11,128,256]{2,1,0:T(8,128)(2,1)S(1)}, u32[]{:S(2)}, u32[]{:S(2)}) %collective-permute-start.6) | collective-permute-done | bytes 720928 | tf_op jit(solution)/shard_map/ppermute | solution.py:587
  143.9 7.7 %collective-permute-done.8.two_ref = bf16[11,128,256]{2,1,0:T(8,128)(2,1)S(1)} collective-permute-done((bf16[11,128,256]{2,1,0:T(8,128)(2,1)S(1)}, bf16[11,128,256]{2,1,0:T(8,128)(2,1)S(1)}, u32[]{:S(2)}, u32[]{:S(2)}) %collective-permute-start.8) | collective-permute-done | bytes 720928 | tf_op jit(solution)/shard_map/ppermute | solution.py:587
  152.0 13.7 %all_to_all.20 = bf16[16,11,16,128]{3,2,1,0:T(8,128)(2,1)S(1)} all-to-all(bf16[16,11,16,128]{3,2,1,0:T(8,128)(2,1)S(1)} %line_sum.1), channel_id=1, replica_groups={{0,8,16,24,32,40,48,56,64,72,80,88,96,104,112,120},{1,9,17,25,3,11,19,2..., dimensions={0} | all-to-all | bytes 1441792 | tf_op jit(solution)/shard_map/all_to_all | solution.py:601
  166.0 16.3 %all_to_all.21.refs_0_ = bf16[16,11,16,128]{3,2,1,0:T(8,128)(2,1)S(1)} all-to-all(bf16[16,11,16,128]{3,2,1,0:T(8,128)(2,1)S(1)} %broadcast_in_dim.16), channel_id=1, replica_groups={{0,8,16,24,32,40,48,56,64,72,80,88,96,104,112,120},{1,9,17,25,3,11,19,2..., dimensions={0} | all-to-all | bytes 1441792 | tf_op jit(solution)/shard_map/all_to_all | solution.py:605
  183.9 1.8 collective-permute-start.10
  185.7 2.7 %collective-permute-start.12 = (bf16[16,11,16,128]{3,2,1,0:T(8,128)(2,1)S(1)}, bf16[16,11,16,128]{3,2,1,0:T(8,128)(2,1)S(1)}, u32[]{:S(2)}, u32[]{:S(2)}) collective-permute-start(bf16[16,11,16,128]{3,2,1,0:T(8,128)(2,1)S(1)} %all_to_all.21.refs_0_), channel_id=1, source_target_pairs={{0,6},{1,97},{2,0},{3,99},{4,2},{5,101},{6,4},{7,103},{8,14},{9,10... | collective-permute-start | bytes 2162696 | tf_op jit(solution)/shard_map/ppermute | solution.py:609
  188.4 2.3 %final_own.1 = (f32[9,474,512]{2,1,0:T(8,128)}, f32[1,512]{1,0:T(1,128)}, f32[512,512]{1,0:T(8,128)}, f32[512,512]{1,0:T(8,128)}) custom-call(s32[4]{0:T(128)S(1)} %broadcast_select_fusion.2.where_ref, bf16[16,11,16,128]{3,2,1,0:T(8,128)(2,1)S(1)} %all_to_all.21.refs_0_, bf16[16,11,16,128]{3,2,1,0:T(8,128)(2,1)S(1)} %collective-permute-done.11.refs_1_), custom_call_target="tpu_custom_call" | custom-call | bytes 4194304 | tf_op jit(solution)/shard_map/final_own/pallas_call | solution.py:619
  190.7 5.2 %collective-permute-done.10.refs_0_ = bf16[16,11,16,128]{3,2,1,0:T(8,128)(2,1)S(1)} collective-permute-done((bf16[16,11,16,128]{3,2,1,0:T(8,128)(2,1)S(1)}, bf16[16,11,16,128]{3,2,1,0:T(8,128)(2,1)S(1)}, u32[]{:S(2)}, u32[]{:S(2)}) %collective-permute-start.10) | collective-permute-done | bytes 720928 | tf_op jit(solution)/shard_map/ppermute | solution.py:609
  196.8 6.8 %collective-permute-done.14.refs_2_ = bf16[16,11,16,128]{3,2,1,0:T(8,128)(2,1)S(1)} collective-permute-done((bf16[16,11,16,128]{3,2,1,0:T(8,128)(2,1)S(1)}, bf16[16,11,16,128]{3,2,1,0:T(8,128)(2,1)S(1)}, u32[]{:S(2)}, u32[]{:S(2)}) %collective-permute-start.14) | collective-permute-done | bytes 720928 | tf_op jit(solution)/shard_map/ppermute | solution.py:609
  204.5 1.7 collective-permute-done.15.refs_3_
  207.3 4.0 %final_line.1 = (f32[9,474,512]{2,1,0:T(8,128)}, f32[1,512]{1,0:T(1,128)}, f32[512,512]{1,0:T(8,128)}, f32[512,512]{1,0:T(8,128)}) custom-call(s32[4]{0:T(128)S(1)} %broadcast_select_fusion.2.where_ref, bf16[16,11,16,128]{3,2,1,0:T(8,128)(2,1)S(1)} %collective-permute-done.10.refs_0_, ...), custom_call_target="tpu_custom_call", output_to_operand_aliasing={{0}: (7, {}), {1}: (8, {}), {2}: (9, {}), {3}: (10, {})} | custom-call | bytes 12582912 | tf_op jit(solution)/shard_map/final_line/pallas_call | solution.py:619
  (84 shorter events, 31.4 us)
Async XLA Ops:
  0.6 41.4 %copy-start = (bf16[512,512]{1,0:T(8,128)(2,1)S(1)}, bf16[512,512]{1,0:T(8,128)(2,1)}, u32[]{:S(2)}) copy-start(bf16[512,512]{1,0:T(8,128)(2,1)} %param.15) | copy-start | bytes 1572868
  1.4 15.6 %collective-permute-start.2 = (bf16[1,1,474]{2,1,0:T(2,128)(2,1)S(1)}, bf16[1,1,474]{2,1,0:T(2,128)(2,1)S(1)}, u32[]{:S(2)}, u32[]{:S(2)}) collective-permute-start(bf16[1,1,474]{2,1,0:T(2,128)(2,1)S(1)} %slice.11), channel_id=1, source_target_pairs={{0,9},{1,10},{2,11},{3,12},{4,13},{5,14},{6,15},{7,8},{8,17},{9,18... | collective-permute-start | bytes 2852 | tf_op jit(solution)/shard_map/ppermute | solution.py:444
  8.1 8.9 %collective-permute-start.1 = (bf16[1,64,474]{2,1,0:T(8,128)(2,1)S(1)}, bf16[1,64,474]{2,1,0:T(8,128)(2,1)S(1)}, u32[]{:S(2)}, u32[]{:S(2)}) collective-permute-start(bf16[1,64,474]{2,1,0:T(8,128)(2,1)S(1)} %slice.10), channel_id=1, source_target_pairs={{0,8},{8,16},{16,24},{24,32},{32,40},{40,48},{48,56},{56,64},{64,7... | collective-permute-start | bytes 182024 | tf_op jit(solution)/shard_map/ppermute | solution.py:443
  12.8 4.2 %collective-permute-start = (bf16[64,1,474]{2,1,0:T(2,128)(2,1)S(1)}, bf16[64,1,474]{2,1,0:T(2,128)(2,1)S(1)}, u32[]{:S(2)}, u32[]{:S(2)}) collective-permute-start(bf16[64,1,474]{2,1,0:T(2,128)(2,1)S(1)} %slice.9), channel_id=1, source_target_pairs={{0,1},{1,2},{2,3},{3,4},{4,5},{5,6},{6,7},{7,0},{8,9},{9,10},{10,1... | collective-permute-start | bytes 182024 | tf_op jit(solution)/shard_map/ppermute | solution.py:440
  32.2 8.1 %copy-start.14 = (s32[1,128,16]{1,2,0:T(8,128)S(1)}, s32[1,128,16]{1,2,0:T(8,128)}, u32[]{:S(2)}) copy-start(s32[1,128,16]{1,2,0:T(8,128)} %param.17) | copy-start | bytes 24580
  32.2 8.8 %copy-start.3 = (bf16[512,512]{1,0:T(8,128)(2,1)S(1)}, bf16[512,512]{1,0:T(8,128)(2,1)}, u32[]{:S(2)}) copy-start(bf16[512,512]{1,0:T(8,128)(2,1)} %w_ref.3) | copy-start | bytes 1572868
  32.2 38.6 %all-to-all-start = ((bf16[128,16,512]{2,1,0:T(8,128)(2,1)}), bf16[128,16,512]{2,1,0:T(8,128)(2,1)S(1)}, u32[]{:S(2)}, u32[]{:S(2)}) async-start(bf16[128,16,512]{2,1,0:T(8,128)(2,1)} %bitcast.28), calls=%async_computation | async-start | bytes 4194304 | tf_op jit(solution)/shard_map/all_to_all | solution.py:497
  77.0 35.8 %all-to-all-start.1 = ((bf16[128,16,512]{2,1,0:T(8,128)(2,1)}), bf16[128,16,512]{2,1,0:T(8,128)(2,1)}, u32[]{:S(2)}, u32[]{:S(2)}) async-start(bf16[128,16,512]{2,1,0:T(8,128)(2,1)} %bitcast.27), calls=%async_computation.1 | async-start | bytes 4194304 | tf_op jit(solution)/shard_map/all_to_all | solution.py:537
  86.3 9.6 %copy-start.5 = (bf16[512,512]{0,1:T(8,128)(2,1)S(1)}, bf16[512,512]{0,1:T(8,128)(2,1)}, u32[]{:S(2)}) copy-start(bf16[512,512]{0,1:T(8,128)(2,1)} %copy.25) | copy-start | bytes 1572868
  125.9 3.3 %collective-permute-start.3 = (bf16[11,128,256]{2,1,0:T(8,128)(2,1)}, bf16[11,128,256]{2,1,0:T(8,128)(2,1)S(1)}, u32[]{:S(2)}, u32[]{:S(2)}) collective-permute-start(bf16[11,128,256]{2,1,0:T(8,128)(2,1)} %get-tuple-element.50), channel_id=1, source_target_pairs={{0,1},{1,0},{2,3},{3,2},{4,5},{5,4},{6,7},{7,6},{8,9},{9,8},{10,11... | collective-permute-start | bytes 2162696 | tf_op jit(solution)/shard_map/ppermute | solution.py:37
  127.1 4.6 %collective-permute-start.5 = (bf16[11,128,256]{2,1,0:T(8,128)(2,1)S(1)}, bf16[11,128,256]{2,1,0:T(8,128)(2,1)S(1)}, u32[]{:S(2)}, u32[]{:S(2)}) collective-permute-start(bf16[11,128,256]{2,1,0:T(8,128)(2,1)S(1)} %get-tuple-element.53), channel_id=1, source_target_pairs={{0,1},{1,0},{2,3},{3,2},{4,5},{5,4},{6,7},{7,6},{8,9},{9,8},{10,11... | collective-permute-start | bytes 2162696 | tf_op jit(solution)/shard_map/ppermute | solution.py:37
  127.2 5.8 %collective-permute-start.7 = (bf16[11,128,256]{2,1,0:T(8,128)(2,1)S(1)}, bf16[11,128,256]{2,1,0:T(8,128)(2,1)S(1)}, u32[]{:S(2)}, u32[]{:S(2)}) collective-permute-start(bf16[11,128,256]{2,1,0:T(8,128)(2,1)S(1)} %get-tuple-element.55), channel_id=1, source_target_pairs={{0,1},{1,0},{2,3},{3,2},{4,5},{5,4},{6,7},{7,6},{8,9},{9,8},{10,11... | collective-permute-start | bytes 2162696 | tf_op jit(solution)/shard_map/ppermute | solution.py:37
  130.6 10.5 %collective-permute-start.9 = (bf16[11,128,256]{2,1,0:T(8,128)(2,1)S(1)}, bf16[11,128,256]{2,1,0:T(8,128)(2,1)S(1)}, u32[]{:S(2)}, u32[]{:S(2)}) collective-permute-start(bf16[11,128,256]{2,1,0:T(8,128)(2,1)S(1)} %add_convert_fusion.2), channel_id=1, source_target_pairs={{0,6},{1,97},{2,0},{3,99},{4,2},{5,101},{6,4},{7,103},{8,14},{9,10... | collective-permute-start | bytes 2162696 | tf_op jit(solution)/shard_map/ppermute | solution.py:587
  131.2 2.4 %collective-permute-start.4 = (bf16[11,128,256]{2,1,0:T(8,128)(2,1)S(1)}, bf16[11,128,256]{2,1,0:T(8,128)(2,1)S(1)}, u32[]{:S(2)}, u32[]{:S(2)}) collective-permute-start(bf16[11,128,256]{2,1,0:T(8,128)(2,1)S(1)} %copy-done.16), channel_id=1, source_target_pairs={{0,1},{1,0},{2,3},{3,2},{4,5},{5,4},{6,7},{7,6},{8,9},{9,8},{10,11... | collective-permute-start | bytes 2162696 | tf_op jit(solution)/shard_map/ppermute | solution.py:37
  131.7 19.9 %copy-start.2 = (bf16[11,128,256]{2,1,0:T(8,128)(2,1)S(1)}, bf16[11,128,256]{2,1,0:T(8,128)(2,1)}, u32[]{:S(2)}) copy-start(bf16[11,128,256]{2,1,0:T(8,128)(2,1)} %get-tuple-element.47.kept_ref) | copy-start | bytes 2162692
  131.8 12.1 %collective-permute-start.6 = (bf16[11,128,256]{2,1,0:T(8,128)(2,1)S(1)}, bf16[11,128,256]{2,1,0:T(8,128)(2,1)S(1)}, u32[]{:S(2)}, u32[]{:S(2)}) collective-permute-start(bf16[11,128,256]{2,1,0:T(8,128)(2,1)S(1)} %add_convert_fusion.1), channel_id=1, source_target_pairs={{0,4},{1,65},{2,6},{3,67},{4,0},{5,69},{6,2},{7,71},{8,12},{9,73},... | collective-permute-start | bytes 2162696 | tf_op jit(solution)/shard_map/ppermute | solution.py:587
  133.1 18.5 %collective-permute-start.8 = (bf16[11,128,256]{2,1,0:T(8,128)(2,1)S(1)}, bf16[11,128,256]{2,1,0:T(8,128)(2,1)S(1)}, u32[]{:S(2)}, u32[]{:S(2)}) collective-permute-start(bf16[11,128,256]{2,1,0:T(8,128)(2,1)S(1)} %add_convert_fusion), channel_id=1, source_target_pairs={{0,2},{1,33},{2,4},{3,35},{4,6},{5,37},{6,0},{7,39},{8,10},{9,41},... | collective-permute-start | bytes 2162696 | tf_op jit(solution)/shard_map/ppermute | solution.py:587
  182.3 6.1 %collective-permute-start.11 = (bf16[16,11,16,128]{3,2,1,0:T(8,128)(2,1)S(1)}, bf16[16,11,16,128]{3,2,1,0:T(8,128)(2,1)S(1)}, u32[]{:S(2)}, u32[]{:S(2)}) collective-permute-start(bf16[16,11,16,128]{3,2,1,0:T(8,128)(2,1)S(1)} %all_to_all.21.refs_0_), channel_id=1, source_target_pairs={{0,1},{1,0},{2,3},{3,2},{4,5},{5,4},{6,7},{7,6},{8,9},{9,8},{10,11... | collective-permute-start | bytes 2162696 | tf_op jit(solution)/shard_map/ppermute | solution.py:37
  183.9 12.0 %collective-permute-start.10 = (bf16[16,11,16,128]{3,2,1,0:T(8,128)(2,1)S(1)}, bf16[16,11,16,128]{3,2,1,0:T(8,128)(2,1)S(1)}, u32[]{:S(2)}, u32[]{:S(2)}) collective-permute-start(bf16[16,11,16,128]{3,2,1,0:T(8,128)(2,1)S(1)} %all_to_all.21.refs_0_), channel_id=1, source_target_pairs={{0,4},{1,65},{2,6},{3,67},{4,0},{5,69},{6,2},{7,71},{8,12},{9,73},... | collective-permute-start | bytes 2162696 | tf_op jit(solution)/shard_map/ppermute | solution.py:609
  185.7 17.8 %collective-permute-start.14 = (bf16[16,11,16,128]{3,2,1,0:T(8,128)(2,1)S(1)}, bf16[16,11,16,128]{3,2,1,0:T(8,128)(2,1)S(1)}, u32[]{:S(2)}, u32[]{:S(2)}) collective-permute-start(bf16[16,11,16,128]{3,2,1,0:T(8,128)(2,1)S(1)} %all_to_all.21.refs_0_), channel_id=1, source_target_pairs={{0,2},{1,33},{2,4},{3,35},{4,6},{5,37},{6,0},{7,39},{8,10},{9,41},... | collective-permute-start | bytes 2162696 | tf_op jit(solution)/shard_map/ppermute | solution.py:609
  185.7 18.7 %collective-permute-start.12 = (bf16[16,11,16,128]{3,2,1,0:T(8,128)(2,1)S(1)}, bf16[16,11,16,128]{3,2,1,0:T(8,128)(2,1)S(1)}, u32[]{:S(2)}, u32[]{:S(2)}) collective-permute-start(bf16[16,11,16,128]{3,2,1,0:T(8,128)(2,1)S(1)} %all_to_all.21.refs_0_), channel_id=1, source_target_pairs={{0,6},{1,97},{2,0},{3,99},{4,2},{5,101},{6,4},{7,103},{8,14},{9,10... | collective-permute-start | bytes 2162696 | tf_op jit(solution)/shard_map/ppermute | solution.py:609
  195.9 8.5 %collective-permute-start.13 = (bf16[16,11,16,128]{3,2,1,0:T(8,128)(2,1)S(1)}, bf16[16,11,16,128]{3,2,1,0:T(8,128)(2,1)S(1)}, u32[]{:S(2)}, u32[]{:S(2)}) collective-permute-start(bf16[16,11,16,128]{3,2,1,0:T(8,128)(2,1)S(1)} %collective-permute-done.10.refs_0_), channel_id=1, source_target_pairs={{0,1},{1,0},{2,3},{3,2},{4,5},{5,4},{6,7},{7,6},{8,9},{9,8},{10,11... | collective-permute-start | bytes 2162696 | tf_op jit(solution)/shard_map/ppermute | solution.py:37
  203.6 2.7 %collective-permute-start.15 = (bf16[16,11,16,128]{3,2,1,0:T(8,128)(2,1)S(1)}, bf16[16,11,16,128]{3,2,1,0:T(8,128)(2,1)S(1)}, u32[]{:S(2)}, u32[]{:S(2)}) collective-permute-start(bf16[16,11,16,128]{3,2,1,0:T(8,128)(2,1)S(1)} %collective-permute-done.14.refs_2_), channel_id=1, source_target_pairs={{0,1},{1,0},{2,3},{3,2},{4,5},{5,4},{6,7},{7,6},{8,9},{9,8},{10,11... | collective-permute-start | bytes 2162696 | tf_op jit(solution)/shard_map/ppermute | solution.py:37
  204.4 2.8 %collective-permute-start.16 = (bf16[16,11,16,128]{3,2,1,0:T(8,128)(2,1)S(1)}, bf16[16,11,16,128]{3,2,1,0:T(8,128)(2,1)S(1)}, u32[]{:S(2)}, u32[]{:S(2)}) collective-permute-start(bf16[16,11,16,128]{3,2,1,0:T(8,128)(2,1)S(1)} %collective-permute-done.12.refs_4_), channel_id=1, source_target_pairs={{0,1},{1,0},{2,3},{3,2},{4,5},{5,4},{6,7},{7,6},{8,9},{9,8},{10,11... | collective-permute-start | bytes 2162696 | tf_op jit(solution)/shard_map/ppermute | solution.py:37
  (12 other events, 28.5 us)

commit v2 on v1

--- a/solution.py
+++ b/solution.py
@@ -3,7 +3,6 @@
 
 import jax
 import jax.numpy as jnp
-import numpy as np
 from jax import lax
 from jax.experimental import pallas as pl
 from jax.experimental.pallas import tpu as pltpu
@@ -78,20 +77,10 @@
     return pl.loop(0, count, unroll=True)
 
 
-def column_picker(image_rows, cols):
-    half = cols // 2
-    out = np.zeros((3, image_rows, half, image_rows, cols), np.float32)
-    lines = [*range(0, image_rows, 2), *range(1, image_rows, 2)]
-    for tap, (place, line), j in itertools.product(range(3), enumerate(lines), range(half)):
-        if 2 * j + tap >= 1:
-            out[tap, place, j, line, 2 * j + tap - 1] = 1.0
-    return jnp.asarray(out.reshape(3 * image_rows * half, image_rows * cols), jnp.bfloat16)
-
-
 def stem_kernel(
-    west_ref, north_ref, corner_ref, picker_ref, north_picker_ref, bias_ref, source_ref,
+    west_ref, north_ref, corner_ref, bias_ref, source_ref,
     grid_hbm, w_hbm, even_hbm, odd_hbm, slope_hbm, out_hbm,
-    grid, raw, weights, even, odd, latent, slope, out, in_sems, w_sems, out_sems, slope_sems, row_sems,
+    grid, wide, raw, weights, even, odd, latent, slope, out, in_sems, w_sems, out_sems, slope_sems, row_sems,
 ):
     rows, cols, channels = grid.shape
     half_rows, half_cols = rows // 2, cols // 2
@@ -112,41 +101,44 @@
     for copy in loads:
         copy.start()
 
-    tail = width - 128
-    even[:, :, :, tail:] = jnp.zeros((3, half_rows, half_cols, 128), bf16)
-    odd[:, :, :, tail:] = jnp.zeros((3, half_rows + 1, half_cols, 128), bf16)
     gap = channels // 16 * 16
     for tap in range(TAPS):
         weights[tap * width + gap : (tap + 1) * width] = jnp.zeros((width - gap, width), bf16)
-    north = f32_dot(north_picker_ref[...], north_ref[0]).astype(bf16)
-    for tap in range(3):
-        odd[tap, 0, :, :channels] = north[tap * half_cols : (tap + 1) * half_cols]
-
+    wide[...] = jnp.zeros_like(wide)
+    edge = 8
+
+    lanes = wide.shape[-1]
+
+    def phases(slot, columns, west, target, line):
+        columns, west = columns.astype(jnp.float32), west.astype(jnp.float32)
+        for number in range(width // lanes):
+            here = slice(number * lanes, min((number + 1) * lanes, channels))
+            held = wide.at[slot, number]
+            held[edge : edge + cols, : here.stop - here.start] = columns[:, here]
+            held[edge - 1 : edge, : here.stop - here.start] = west[:, here]
+            for tap in range(3):
+                taken = wide[slot, number, pl.ds(edge - 1 + tap, half_cols, stride=2), :]
+                target[tap, line, :, number * lanes : (number + 1) * lanes] = taken.astype(bf16)
+
+    phases(0, north_ref[0], corner_ref[0], odd, 0)
+    slots_wide = wide.shape[0]
     for chunk in range(chunks):
         loads[chunk].wait()
         if chunk == chunks - 2:
             for copy in w_loads:
                 copy.start()
 
-        @unrolled(per_chunk // 4)
+        @unrolled(per_chunk // slots_wide)
         def _(step):
-            group = chunk * (per_chunk // 4) + step
-            block = grid[pl.ds(4 * group, 4)].reshape(4 * cols, channels)
-            picked = f32_dot(picker_ref[...], block).astype(bf16)
-            picked = picked.reshape(3, 2, 2, half_cols, channels)
-            for tap in range(3):
-                even[tap, pl.ds(2 * group, 2), :, :channels] = picked[tap, 0]
-                odd[tap, pl.ds(2 * group + 1, 2), :, :channels] = picked[tap, 1]
-
-    def patch(target, first, count, column):
-        old = target[0, first : first + count, 0:16, :channels].astype(jnp.float32)
-        line = lax.broadcasted_iota(jnp.int32, old.shape, 1)
-        new = jnp.where(line == 0, column.astype(jnp.float32), old)
-        target[0, first : first + count, 0:16, :channels] = new.astype(bf16)
-
-    patch(even, 0, half_rows, west_ref[:, 0])
-    patch(odd, 1, half_rows, west_ref[:, 1])
-    patch(odd, 0, 1, corner_ref[...])
+            first = chunk * per_chunk + slots_wide * step
+            pair = chunk * (per_chunk // 2) + (slots_wide // 2) * step
+            for slot in range(slots_wide):
+                target = odd if slot % 2 else even
+                phases(
+                    slot, grid[first + slot], west_ref[first + slot], target,
+                    pair + slot // 2 + slot % 2,
+                )
+
     phase_copies = [
         pltpu.make_async_copy(even, even_hbm, out_sems.at[0]),
         pltpu.make_async_copy(odd, odd_hbm, out_sems.at[1]),
@@ -224,9 +216,10 @@
         write(odd_ref[col_tap, pl.ds(row_tap // 2, half_rows)])
 
 
-def edge_kernel(side, w_ref, flipped_ref, dst_ref, agg_ref, rows_hbm, *refs):
+def edge_kernel(side, w_ref, dst_ref, agg_ref, rows_hbm, *refs):
     outs = 2 if side else 1
-    placed, (rows, *kept), (in_sems, out_sems) = refs[:outs], refs[outs : 2 * outs + 1], refs[2 * outs + 1 :]
+    placed, (rows, *kept) = refs[:outs], refs[outs : 2 * outs + 1]
+    flipped_ref, in_sems, out_sems = refs[2 * outs + 1 :]
     nodes = agg_ref.shape[0]
     tiles = in_sems.shape[0]
     tile = rows.shape[0] // tiles
@@ -244,6 +237,8 @@
         ]
 
     load(0).start()
+    if not side:
+        flipped_ref[...] = w_ref[...].T
 
     @unrolled(tiles)
     def _(step):
@@ -463,10 +458,11 @@
             pltpu.HBM((points, width), f32),
             pltpu.HBM((slots, width), bf16),
         ),
-        in_specs=[whole()] * 7 + [whole(pltpu.HBM)] * 2,
+        in_specs=[whole()] * 5 + [whole(pltpu.HBM)] * 2,
         out_specs=(whole(pltpu.HBM),) * 4,
         scratch_shapes=[
             pltpu.VMEM((rows_here, cols_here, channels), bf16),
+            pltpu.VMEM((4, width // 128, cols_here + 16, 128), f32),
             pltpu.VMEM((TAPS, channels, width), bf16),
             pltpu.VMEM((TAPS * width, width), bf16),
             pltpu.VMEM((3, half_rows, half_cols, width), bf16),
@@ -483,11 +479,9 @@
         compiler_params=params(56),
         name="stem",
     )(
-        west.reshape(half_rows, 2, 1, channels),
+        west,
         north,
         corner,
-        column_picker(4, cols_here),
-        column_picker(1, cols_here),
         b_stem.reshape(1, width),
         source.reshape(slots, 1),
         grid_input,
@@ -516,21 +510,21 @@
     dst_flat = dst_index.reshape(slots)
 
     dst_row = dst_flat.reshape(1, slots)
-    w_flipped = w_edge.T
 
     def edge_call(side):
         outs = 2 if side else 1
         return pl.pallas_call(
             functools.partial(edge_kernel, side),
             out_shape=(pltpu.HBM((slots, width), bf16),) * outs,
-            in_specs=[whole()] * 4 + [whole(pltpu.HBM)],
+            in_specs=[whole()] * 3 + [whole(pltpu.HBM)],
             out_specs=(whole(pltpu.HBM),) * outs,
             scratch_shapes=[pltpu.VMEM((slots, width), bf16)] * (1 + outs)
+            + [pltpu.VMEM((width, width), bf16)]
             + [pltpu.SemaphoreType.DMA((2,)), pltpu.SemaphoreType.DMA((outs, 2))],
             compiler_params=params(40),
             cost_estimate=cost(4 * slots * width * width, 8 * MIB),
             name="edge_side" if side else "edge_back",
-        )(w_edge, w_flipped, dst_row, grad_agg, arrived)
+        )(w_edge, dst_row, grad_agg, arrived)
 
     (back,) = edge_call(False)
 

time: 212 us -> 211 us (level)
  local copies, waits for them, and re-layouts: 11.6 us -> 6.85 us
  waiting for transfers between devices: 68 us -> 72.4 us
    all_to_all x1, waiting for transfers between devices: 6.18 us -> 9.66 us  [shards(): lax.all_to_all(back.reshape(device_count, slot_count, width), EVERY, spli...]
    unnamed x37 -> x38, local copies, waits for them, and re-layouts: 4.36 us -> 2.42 us
  transfers between devices with their start and end apart: 19 -> 19, of which waited for: 10 -> 10; matrix products, arithmetic and copies ran while one was open for 9% -> 7% of each run, Pallas kernels for 8% -> 8%
where the time goes in v2:
time: 211 us; the launch traced here: 210 us
  waiting for transfers between devices  72.4 us (34%)
  Pallas kernels  53.9 us (26%)
  starting transfers between devices  35.6 us (17%)
  blocking collectives  30 us (14%)
  local copies, waits for them, and re-layouts  6.85 us (3%)
  matrix products  6.62 us (3%)
  other arithmetic  3.73 us (2%)
    all_to_all x1, waiting for transfers between devices, shards(): lax.all_to_all(outgoing.reshape(device_count, slot_count, width), EVERY,...  28.3 us
    ppermute x3, waiting for transfers between devices, shards(): lax.ppermute(chip_sum, EVERY, line_pairs(step))  18 us
    all_to_all x1, blocking collectives, shards(): lax.all_to_all(jnp.broadcast_to(summed[None], part), EVERY, split_axis=0,...  16.3 us
    pallas_call x1, Pallas kernels, shards(): pl.pallas_call(stem_kernel, out_shape=(pltpu.HBM((3, half_rows, half_cols...  14.1 us
    all_to_all x1, blocking collectives, shards(): lax.all_to_all(line_sum, EVERY, split_axis=0, concat_axis=0, tiled=True,...  13.7 us
    pallas_call x1, Pallas kernels, shards(): pl.pallas_call(gradients_kernel, out_shape=(jax.ShapeDtypeStruct(quarter_...  13.1 us
    ppermute x3, waiting for transfers between devices, shards(): held = [lax.ppermute(mine, EVERY, line_pairs(step)) for step in steps_out]  12 us
    pallas_call x2, Pallas kernels, edge_call(): pl.pallas_call(functools.partial(edge_kernel, side), out_shape=(pltpu.HBM...  10.3 us
  transfers between devices with their start and end apart: 19, of which 10 were waited for; matrix products, arithmetic and copies ran while one was open for 7% of the time, Pallas kernels for 8%

profile of v2, /device:TPU:1, one launch (start us, length us, event | category | flops | bytes accessed | tf_op | source)
XLA Modules:
  0.0 210.2 jit_solution(6000392237333903630)
XLA Ops:
  1.4 5.8 %collective-permute-start.2 = (bf16[1,1,474]{2,1,0:T(2,128)(2,1)S(1)}, bf16[1,1,474]{2,1,0:T(2,128)(2,1)S(1)}, u32[]{:S(2)}, u32[]{:S(2)}) collective-permute-start(bf16[1,1,474]{2,1,0:T(2,128)(2,1)S(1)} %slice.11), channel_id=1, source_target_pairs={{0,9},{1,10},{2,11},{3,12},{4,13},{5,14},{6,15},{7,8},{8,17},{9,18... | collective-permute-start | bytes 2852 | tf_op jit(solution)/shard_map/ppermute | solution.py:439
  8.1 3.5 %collective-permute-start.1 = (bf16[1,64,474]{2,1,0:T(8,128)(2,1)S(1)}, bf16[1,64,474]{2,1,0:T(8,128)(2,1)S(1)}, u32[]{:S(2)}, u32[]{:S(2)}) collective-permute-start(bf16[1,64,474]{2,1,0:T(8,128)(2,1)S(1)} %slice.10), channel_id=1, source_target_pairs={{0,8},{8,16},{16,24},{24,32},{32,40},{40,48},{48,56},{56,64},{64,7... | collective-permute-start | bytes 182024 | tf_op jit(solution)/shard_map/ppermute | solution.py:438
  17.7 14.1 %stem.1 = (bf16[3,32,32,512]{3,2,1,0:T(8,128)(2,1)}, bf16[3,33,32,512]{3,2,1,0:T(8,128)(2,1)}, f32[1024,512]{1,0:T(8,128)}, bf16[2048,512]{1,0:T(8,128)(2,1)}) custom-call(bf16[64,1,474]{2,1,0:T(2,128)(2,1)} %copy-done.13, bf16[1,64,474]{2,1,0:T(8,128)(2,1)} %copy-done.14, bf16[1,1,474]{2,1,0:T(2,128)(2,1)} %copy-done.16, f32[1,512]{1,0:T(1,128)} %bitcast.25, ...), custom_call_target="tpu_custom_call" | custom-call | tf_op jit(solution)/shard_map/stem/pallas_call | solution.py:453
  31.8 8.0 %all-to-all-start = ((bf16[128,16,512]{2,1,0:T(8,128)(2,1)}), bf16[128,16,512]{2,1,0:T(8,128)(2,1)S(1)}, u32[]{:S(2)}, u32[]{:S(2)}) async-start(bf16[128,16,512]{2,1,0:T(8,128)(2,1)} %bitcast.24), calls=%async_computation | async-start | bytes 4194304 | tf_op jit(solution)/shard_map/all_to_all | solution.py:491
  42.0 28.3 %all-to-all-done = bf16[128,16,512]{2,1,0:T(8,128)(2,1)S(1)} async-done(((bf16[128,16,512]{2,1,0:T(8,128)(2,1)}), bf16[128,16,512]{2,1,0:T(8,128)(2,1)S(1)}, u32[]{:S(2)}, u32[]{:S(2)}) %all-to-all-start) | async-done | bytes 2097184 | tf_op jit(solution)/shard_map/all_to_all | solution.py:491
  70.3 5.2 %edge_back.1 = bf16[2048,512]{1,0:T(8,128)(2,1)} custom-call(bf16[512,512]{1,0:T(8,128)(2,1)S(1)} %copy-done.3, s32[1,2048]{1,0:T(1,128)S(1)} %broadcast_in_dim_reshape.3.dst_ref, bf16[320,512]{1,0:T(8,128)(2,1)S(1)} %convolution_convert_fusion.3.agg_ref, bf16[2048,512]{1,0:T(8,128)(2,1)S(1)} %bitcast.20), custom_call_target="tpu_custom_call" | custom-call | flops 2147483648 | bytes 8388608 | tf_op jit(solution)/shard_map/edge_back/pallas_call | solution.py:516
  75.6 5.5 %all-to-all-start.1 = ((bf16[128,16,512]{2,1,0:T(8,128)(2,1)}), bf16[128,16,512]{2,1,0:T(8,128)(2,1)}, u32[]{:S(2)}, u32[]{:S(2)}) async-start(bf16[128,16,512]{2,1,0:T(8,128)(2,1)} %bitcast.23), calls=%async_computation.1 | async-start | bytes 4194304 | tf_op jit(solution)/shard_map/all_to_all | solution.py:531
  81.6 9.6 %flip.1.patches_hbm = bf16[9,512,1024]{2,1,0:T(8,128)(2,1)} custom-call(bf16[3,32,32,512]{3,2,1,0:T(8,128)(2,1)} %get-tuple-element.45.even_ref, bf16[3,33,32,512]{3,2,1,0:T(8,128)(2,1)} %get-tuple-element.46.odd_ref), custom_call_target="tpu_custom_call" | custom-call | bytes 16777216 | tf_op jit(solution)/shard_map/flip/pallas_call | solution.py:496
  91.2 5.1 %edge_side.1 = (bf16[2048,512]{1,0:T(8,128)(2,1)}, bf16[2048,512]{1,0:T(8,128)(2,1)}) custom-call(bf16[512,512]{1,0:T(8,128)(2,1)S(1)} %copy-done.4, s32[1,2048]{1,0:T(1,128)S(1)} %broadcast_in_dim_reshape.3.dst_ref, bf16[320,512]{1,0:T(8,128)(2,1)S(1)} %convolution_convert_fusion.3.agg_ref, bf16[2048,512]{1,0:T(8,128)(2,1)S(1)} %bitcast.21), custom_call_target="tpu_custom_call" | custom-call | flops 2147483648 | bytes 8388608 | tf_op jit(solution)/shard_map/edge_side/pallas_call | solution.py:516
  96.3 2.5 %fusion.2 = bf16[320,512]{1,0:T(8,128)(2,1)S(1)} fusion(bf16[2048,512]{1,0:T(8,128)(2,1)} %get-tuple-element.39, s32[2048]{0:T(1024)S(1)} %eq.19), kind=kOutput, calls=%fused_computation.8 | convolution fusion | flops 671907840 | bytes 2433024 | tf_op jit(solution)/shard_map/dot_general | solution.py:20
  101.8 9.7 %all-to-all-done.1 = bf16[128,16,512]{2,1,0:T(8,128)(2,1)} async-done(((bf16[128,16,512]{2,1,0:T(8,128)(2,1)}), bf16[128,16,512]{2,1,0:T(8,128)(2,1)}, u32[]{:S(2)}, u32[]{:S(2)}) %all-to-all-start.1) | async-done | bytes 2097184 | tf_op jit(solution)/shard_map/all_to_all | solution.py:531
  111.5 13.1 %gradients.1 = (bf16[11,128,256]{2,1,0:T(8,128)(2,1)S(1)}, bf16[11,128,256]{2,1,0:T(8,128)(2,1)S(1)}, bf16[11,128,256]{2,1,0:T(8,128)(2,1)}, bf16[11,128,256]{2,...) custom-call(s32[4]{0:T(128)S(1)} %broadcast_select_fusion.2.where_re, ...), custom_call_target="tpu_custom_call" | custom-call | tf_op jit(solution)/shard_map/gradients/pallas_call | solution.py:553
  132.3 7.5 %collective-permute-done.9.three_ref = bf16[11,128,256]{2,1,0:T(8,128)(2,1)S(1)} collective-permute-done((bf16[11,128,256]{2,1,0:T(8,128)(2,1)S(1)}, bf16[11,128,256]{2,1,0:T(8,128)(2,1)S(1)}, u32[]{:S(2)}, u32[]{:S(2)}) %collective-permute-start.9) | collective-permute-done | bytes 720928 | tf_op jit(solution)/shard_map/ppermute | solution.py:581
  139.8 2.8 %collective-permute-done.6.one_ref = bf16[11,128,256]{2,1,0:T(8,128)(2,1)S(1)} collective-permute-done((bf16[11,128,256]{2,1,0:T(8,128)(2,1)S(1)}, bf16[11,128,256]{2,1,0:T(8,128)(2,1)S(1)}, u32[]{:S(2)}, u32[]{:S(2)}) %collective-permute-start.6) | collective-permute-done | bytes 720928 | tf_op jit(solution)/shard_map/ppermute | solution.py:581
  142.6 7.7 %collective-permute-done.8.two_ref = bf16[11,128,256]{2,1,0:T(8,128)(2,1)S(1)} collective-permute-done((bf16[11,128,256]{2,1,0:T(8,128)(2,1)S(1)}, bf16[11,128,256]{2,1,0:T(8,128)(2,1)S(1)}, u32[]{:S(2)}, u32[]{:S(2)}) %collective-permute-start.8) | collective-permute-done | bytes 720928 | tf_op jit(solution)/shard_map/ppermute | solution.py:581
  150.8 13.7 %all_to_all.20 = bf16[16,11,16,128]{3,2,1,0:T(8,128)(2,1)S(1)} all-to-all(bf16[16,11,16,128]{3,2,1,0:T(8,128)(2,1)S(1)} %line_sum.1), channel_id=1, replica_groups={{0,8,16,24,32,40,48,56,64,72,80,88,96,104,112,120},{1,9,17,25,3,11,19,2..., dimensions={0} | all-to-all | bytes 1441792 | tf_op jit(solution)/shard_map/all_to_all | solution.py:595
  164.7 16.3 %all_to_all.21.refs_0_ = bf16[16,11,16,128]{3,2,1,0:T(8,128)(2,1)S(1)} all-to-all(bf16[16,11,16,128]{3,2,1,0:T(8,128)(2,1)S(1)} %broadcast_in_dim.16), channel_id=1, replica_groups={{0,8,16,24,32,40,48,56,64,72,80,88,96,104,112,120},{1,9,17,25,3,11,19,2..., dimensions={0} | all-to-all | bytes 1441792 | tf_op jit(solution)/shard_map/all_to_all | solution.py:599
  182.6 1.8 collective-permute-start.10
  184.5 2.7 %collective-permute-start.12 = (bf16[16,11,16,128]{3,2,1,0:T(8,128)(2,1)S(1)}, bf16[16,11,16,128]{3,2,1,0:T(8,128)(2,1)S(1)}, u32[]{:S(2)}, u32[]{:S(2)}) collective-permute-start(bf16[16,11,16,128]{3,2,1,0:T(8,128)(2,1)S(1)} %all_to_all.21.refs_0_), channel_id=1, source_target_pairs={{0,6},{1,97},{2,0},{3,99},{4,2},{5,101},{6,4},{7,103},{8,14},{9,10... | collective-permute-start | bytes 2162696 | tf_op jit(solution)/shard_map/ppermute | solution.py:603
  187.1 2.3 %final_own.1 = (f32[9,474,512]{2,1,0:T(8,128)}, f32[1,512]{1,0:T(1,128)}, f32[512,512]{1,0:T(8,128)}, f32[512,512]{1,0:T(8,128)}) custom-call(s32[4]{0:T(128)S(1)} %broadcast_select_fusion.2.where_ref, bf16[16,11,16,128]{3,2,1,0:T(8,128)(2,1)S(1)} %all_to_all.21.refs_0_, bf16[16,11,16,128]{3,2,1,0:T(8,128)(2,1)S(1)} %collective-permute-done.11.refs_1_), custom_call_target="tpu_custom_call" | custom-call | bytes 4194304 | tf_op jit(solution)/shard_map/final_own/pallas_call | solution.py:613
  189.4 5.2 %collective-permute-done.10.refs_0_ = bf16[16,11,16,128]{3,2,1,0:T(8,128)(2,1)S(1)} collective-permute-done((bf16[16,11,16,128]{3,2,1,0:T(8,128)(2,1)S(1)}, bf16[16,11,16,128]{3,2,1,0:T(8,128)(2,1)S(1)}, u32[]{:S(2)}, u32[]{:S(2)}) %collective-permute-start.10) | collective-permute-done | bytes 720928 | tf_op jit(solution)/shard_map/ppermute | solution.py:603
  195.5 6.8 %collective-permute-done.14.refs_2_ = bf16[16,11,16,128]{3,2,1,0:T(8,128)(2,1)S(1)} collective-permute-done((bf16[16,11,16,128]{3,2,1,0:T(8,128)(2,1)S(1)}, bf16[16,11,16,128]{3,2,1,0:T(8,128)(2,1)S(1)}, u32[]{:S(2)}, u32[]{:S(2)}) %collective-permute-start.14) | collective-permute-done | bytes 720928 | tf_op jit(solution)/shard_map/ppermute | solution.py:603
  203.3 1.7 collective-permute-done.15.refs_3_
  206.0 4.0 %final_line.1 = (f32[9,474,512]{2,1,0:T(8,128)}, f32[1,512]{1,0:T(1,128)}, f32[512,512]{1,0:T(8,128)}, f32[512,512]{1,0:T(8,128)}) custom-call(s32[4]{0:T(128)S(1)} %broadcast_select_fusion.2.where_ref, bf16[16,11,16,128]{3,2,1,0:T(8,128)(2,1)S(1)} %collective-permute-done.10.refs_0_, ...), custom_call_target="tpu_custom_call", output_to_operand_aliasing={{0}: (7, {}), {1}: (8, {}), {2}: (9, {}), {3}: (10, {})} | custom-call | bytes 12582912 | tf_op jit(solution)/shard_map/final_line/pallas_call | solution.py:613
  (85 shorter events, 26.0 us)
Async XLA Ops:
  0.6 40.0 %copy-start = (bf16[512,512]{1,0:T(8,128)(2,1)S(1)}, bf16[512,512]{1,0:T(8,128)(2,1)}, u32[]{:S(2)}) copy-start(bf16[512,512]{1,0:T(8,128)(2,1)} %param.13) | copy-start | bytes 1572868
  1.4 15.6 %collective-permute-start.2 = (bf16[1,1,474]{2,1,0:T(2,128)(2,1)S(1)}, bf16[1,1,474]{2,1,0:T(2,128)(2,1)S(1)}, u32[]{:S(2)}, u32[]{:S(2)}) collective-permute-start(bf16[1,1,474]{2,1,0:T(2,128)(2,1)S(1)} %slice.11), channel_id=1, source_target_pairs={{0,9},{1,10},{2,11},{3,12},{4,13},{5,14},{6,15},{7,8},{8,17},{9,18... | collective-permute-start | bytes 2852 | tf_op jit(solution)/shard_map/ppermute | solution.py:439
  8.1 8.9 %collective-permute-start.1 = (bf16[1,64,474]{2,1,0:T(8,128)(2,1)S(1)}, bf16[1,64,474]{2,1,0:T(8,128)(2,1)S(1)}, u32[]{:S(2)}, u32[]{:S(2)}) collective-permute-start(bf16[1,64,474]{2,1,0:T(8,128)(2,1)S(1)} %slice.10), channel_id=1, source_target_pairs={{0,8},{8,16},{16,24},{24,32},{32,40},{40,48},{48,56},{56,64},{64,7... | collective-permute-start | bytes 182024 | tf_op jit(solution)/shard_map/ppermute | solution.py:438
  12.8 4.2 %collective-permute-start = (bf16[64,1,474]{2,1,0:T(2,128)(2,1)S(1)}, bf16[64,1,474]{2,1,0:T(2,128)(2,1)S(1)}, u32[]{:S(2)}, u32[]{:S(2)}) collective-permute-start(bf16[64,1,474]{2,1,0:T(2,128)(2,1)S(1)} %slice.9), channel_id=1, source_target_pairs={{0,1},{1,2},{2,3},{3,4},{4,5},{5,6},{6,7},{7,0},{8,9},{9,10},{10,1... | collective-permute-start | bytes 182024 | tf_op jit(solution)/shard_map/ppermute | solution.py:435
  31.8 8.1 %copy-start.15 = (s32[1,128,16]{1,2,0:T(8,128)S(1)}, s32[1,128,16]{1,2,0:T(8,128)}, u32[]{:S(2)}) copy-start(s32[1,128,16]{1,2,0:T(8,128)} %param.15) | copy-start | bytes 24580
  31.8 38.6 %copy-start.3 = (bf16[512,512]{1,0:T(8,128)(2,1)S(1)}, bf16[512,512]{1,0:T(8,128)(2,1)}, u32[]{:S(2)}) copy-start(bf16[512,512]{1,0:T(8,128)(2,1)} %w_ref.3) | copy-start | bytes 1572868
  31.8 38.6 %all-to-all-start = ((bf16[128,16,512]{2,1,0:T(8,128)(2,1)}), bf16[128,16,512]{2,1,0:T(8,128)(2,1)S(1)}, u32[]{:S(2)}, u32[]{:S(2)}) async-start(bf16[128,16,512]{2,1,0:T(8,128)(2,1)} %bitcast.24), calls=%async_computation | async-start | bytes 4194304 | tf_op jit(solution)/shard_map/all_to_all | solution.py:491
  75.6 35.9 %all-to-all-start.1 = ((bf16[128,16,512]{2,1,0:T(8,128)(2,1)}), bf16[128,16,512]{2,1,0:T(8,128)(2,1)}, u32[]{:S(2)}, u32[]{:S(2)}) async-start(bf16[128,16,512]{2,1,0:T(8,128)(2,1)} %bitcast.23), calls=%async_computation.1 | async-start | bytes 4194304 | tf_op jit(solution)/shard_map/all_to_all | solution.py:531
  81.6 9.6 %copy-start.4 = (bf16[512,512]{1,0:T(8,128)(2,1)S(1)}, bf16[512,512]{1,0:T(8,128)(2,1)}, u32[]{:S(2)}) copy-start(bf16[512,512]{1,0:T(8,128)(2,1)} %w_ref.3) | copy-start | bytes 1572868
  124.6 3.3 %collective-permute-start.3 = (bf16[11,128,256]{2,1,0:T(8,128)(2,1)}, bf16[11,128,256]{2,1,0:T(8,128)(2,1)S(1)}, u32[]{:S(2)}, u32[]{:S(2)}) collective-permute-start(bf16[11,128,256]{2,1,0:T(8,128)(2,1)} %get-tuple-element.50), channel_id=1, source_target_pairs={{0,1},{1,0},{2,3},{3,2},{4,5},{5,4},{6,7},{7,6},{8,9},{9,8},{10,11... | collective-permute-start | bytes 2162696 | tf_op jit(solution)/shard_map/ppermute | solution.py:36
  125.8 4.6 %collective-permute-start.5 = (bf16[11,128,256]{2,1,0:T(8,128)(2,1)S(1)}, bf16[11,128,256]{2,1,0:T(8,128)(2,1)S(1)}, u32[]{:S(2)}, u32[]{:S(2)}) collective-permute-start(bf16[11,128,256]{2,1,0:T(8,128)(2,1)S(1)} %get-tuple-element.53), channel_id=1, source_target_pairs={{0,1},{1,0},{2,3},{3,2},{4,5},{5,4},{6,7},{7,6},{8,9},{9,8},{10,11... | collective-permute-start | bytes 2162696 | tf_op jit(solution)/shard_map/ppermute | solution.py:36
  125.9 5.8 %collective-permute-start.7 = (bf16[11,128,256]{2,1,0:T(8,128)(2,1)S(1)}, bf16[11,128,256]{2,1,0:T(8,128)(2,1)S(1)}, u32[]{:S(2)}, u32[]{:S(2)}) collective-permute-start(bf16[11,128,256]{2,1,0:T(8,128)(2,1)S(1)} %get-tuple-element.55), channel_id=1, source_target_pairs={{0,1},{1,0},{2,3},{3,2},{4,5},{5,4},{6,7},{7,6},{8,9},{9,8},{10,11... | collective-permute-start | bytes 2162696 | tf_op jit(solution)/shard_map/ppermute | solution.py:36
  129.3 10.5 %collective-permute-start.9 = (bf16[11,128,256]{2,1,0:T(8,128)(2,1)S(1)}, bf16[11,128,256]{2,1,0:T(8,128)(2,1)S(1)}, u32[]{:S(2)}, u32[]{:S(2)}) collective-permute-start(bf16[11,128,256]{2,1,0:T(8,128)(2,1)S(1)} %add_convert_fusion.2), channel_id=1, source_target_pairs={{0,6},{1,97},{2,0},{3,99},{4,2},{5,101},{6,4},{7,103},{8,14},{9,10... | collective-permute-start | bytes 2162696 | tf_op jit(solution)/shard_map/ppermute | solution.py:581
  129.9 2.4 %collective-permute-start.4 = (bf16[11,128,256]{2,1,0:T(8,128)(2,1)S(1)}, bf16[11,128,256]{2,1,0:T(8,128)(2,1)S(1)}, u32[]{:S(2)}, u32[]{:S(2)}) collective-permute-start(bf16[11,128,256]{2,1,0:T(8,128)(2,1)S(1)} %copy-done.17), channel_id=1, source_target_pairs={{0,1},{1,0},{2,3},{3,2},{4,5},{5,4},{6,7},{7,6},{8,9},{9,8},{10,11... | collective-permute-start | bytes 2162696 | tf_op jit(solution)/shard_map/ppermute | solution.py:36
  130.4 19.9 %copy-start.2 = (bf16[11,128,256]{2,1,0:T(8,128)(2,1)S(1)}, bf16[11,128,256]{2,1,0:T(8,128)(2,1)}, u32[]{:S(2)}) copy-start(bf16[11,128,256]{2,1,0:T(8,128)(2,1)} %get-tuple-element.47.kept_ref) | copy-start | bytes 2162692
  130.6 12.1 %collective-permute-start.6 = (bf16[11,128,256]{2,1,0:T(8,128)(2,1)S(1)}, bf16[11,128,256]{2,1,0:T(8,128)(2,1)S(1)}, u32[]{:S(2)}, u32[]{:S(2)}) collective-permute-start(bf16[11,128,256]{2,1,0:T(8,128)(2,1)S(1)} %add_convert_fusion.1), channel_id=1, source_target_pairs={{0,4},{1,65},{2,6},{3,67},{4,0},{5,69},{6,2},{7,71},{8,12},{9,73},... | collective-permute-start | bytes 2162696 | tf_op jit(solution)/shard_map/ppermute | solution.py:581
  131.9 18.5 %collective-permute-start.8 = (bf16[11,128,256]{2,1,0:T(8,128)(2,1)S(1)}, bf16[11,128,256]{2,1,0:T(8,128)(2,1)S(1)}, u32[]{:S(2)}, u32[]{:S(2)}) collective-permute-start(bf16[11,128,256]{2,1,0:T(8,128)(2,1)S(1)} %add_convert_fusion), channel_id=1, source_target_pairs={{0,2},{1,33},{2,4},{3,35},{4,6},{5,37},{6,0},{7,39},{8,10},{9,41},... | collective-permute-start | bytes 2162696 | tf_op jit(solution)/shard_map/ppermute | solution.py:581
  181.0 6.1 %collective-permute-start.11 = (bf16[16,11,16,128]{3,2,1,0:T(8,128)(2,1)S(1)}, bf16[16,11,16,128]{3,2,1,0:T(8,128)(2,1)S(1)}, u32[]{:S(2)}, u32[]{:S(2)}) collective-permute-start(bf16[16,11,16,128]{3,2,1,0:T(8,128)(2,1)S(1)} %all_to_all.21.refs_0_), channel_id=1, source_target_pairs={{0,1},{1,0},{2,3},{3,2},{4,5},{5,4},{6,7},{7,6},{8,9},{9,8},{10,11... | collective-permute-start | bytes 2162696 | tf_op jit(solution)/shard_map/ppermute | solution.py:36
  182.6 12.0 %collective-permute-start.10 = (bf16[16,11,16,128]{3,2,1,0:T(8,128)(2,1)S(1)}, bf16[16,11,16,128]{3,2,1,0:T(8,128)(2,1)S(1)}, u32[]{:S(2)}, u32[]{:S(2)}) collective-permute-start(bf16[16,11,16,128]{3,2,1,0:T(8,128)(2,1)S(1)} %all_to_all.21.refs_0_), channel_id=1, source_target_pairs={{0,4},{1,65},{2,6},{3,67},{4,0},{5,69},{6,2},{7,71},{8,12},{9,73},... | collective-permute-start | bytes 2162696 | tf_op jit(solution)/shard_map/ppermute | solution.py:603
  184.5 17.8 %collective-permute-start.14 = (bf16[16,11,16,128]{3,2,1,0:T(8,128)(2,1)S(1)}, bf16[16,11,16,128]{3,2,1,0:T(8,128)(2,1)S(1)}, u32[]{:S(2)}, u32[]{:S(2)}) collective-permute-start(bf16[16,11,16,128]{3,2,1,0:T(8,128)(2,1)S(1)} %all_to_all.21.refs_0_), channel_id=1, source_target_pairs={{0,2},{1,33},{2,4},{3,35},{4,6},{5,37},{6,0},{7,39},{8,10},{9,41},... | collective-permute-start | bytes 2162696 | tf_op jit(solution)/shard_map/ppermute | solution.py:603
  184.5 18.7 %collective-permute-start.12 = (bf16[16,11,16,128]{3,2,1,0:T(8,128)(2,1)S(1)}, bf16[16,11,16,128]{3,2,1,0:T(8,128)(2,1)S(1)}, u32[]{:S(2)}, u32[]{:S(2)}) collective-permute-start(bf16[16,11,16,128]{3,2,1,0:T(8,128)(2,1)S(1)} %all_to_all.21.refs_0_), channel_id=1, source_target_pairs={{0,6},{1,97},{2,0},{3,99},{4,2},{5,101},{6,4},{7,103},{8,14},{9,10... | collective-permute-start | bytes 2162696 | tf_op jit(solution)/shard_map/ppermute | solution.py:603
  194.6 8.5 %collective-permute-start.13 = (bf16[16,11,16,128]{3,2,1,0:T(8,128)(2,1)S(1)}, bf16[16,11,16,128]{3,2,1,0:T(8,128)(2,1)S(1)}, u32[]{:S(2)}, u32[]{:S(2)}) collective-permute-start(bf16[16,11,16,128]{3,2,1,0:T(8,128)(2,1)S(1)} %collective-permute-done.10.refs_0_), channel_id=1, source_target_pairs={{0,1},{1,0},{2,3},{3,2},{4,5},{5,4},{6,7},{7,6},{8,9},{9,8},{10,11... | collective-permute-start | bytes 2162696 | tf_op jit(solution)/shard_map/ppermute | solution.py:36
  202.3 2.7 %collective-permute-start.15 = (bf16[16,11,16,128]{3,2,1,0:T(8,128)(2,1)S(1)}, bf16[16,11,16,128]{3,2,1,0:T(8,128)(2,1)S(1)}, u32[]{:S(2)}, u32[]{:S(2)}) collective-permute-start(bf16[16,11,16,128]{3,2,1,0:T(8,128)(2,1)S(1)} %collective-permute-done.14.refs_2_), channel_id=1, source_target_pairs={{0,1},{1,0},{2,3},{3,2},{4,5},{5,4},{6,7},{7,6},{8,9},{9,8},{10,11... | collective-permute-start | bytes 2162696 | tf_op jit(solution)/shard_map/ppermute | solution.py:36
  203.2 2.8 %collective-permute-start.16 = (bf16[16,11,16,128]{3,2,1,0:T(8,128)(2,1)S(1)}, bf16[16,11,16,128]{3,2,1,0:T(8,128)(2,1)S(1)}, u32[]{:S(2)}, u32[]{:S(2)}) collective-permute-start(bf16[16,11,16,128]{3,2,1,0:T(8,128)(2,1)S(1)} %collective-permute-done.12.refs_4_), channel_id=1, source_target_pairs={{0,1},{1,0},{2,3},{3,2},{4,5},{5,4},{6,7},{7,6},{8,9},{9,8},{10,11... | collective-permute-start | bytes 2162696 | tf_op jit(solution)/shard_map/ppermute | solution.py:36
  (13 other events, 38.9 us)

commit v3 on v2

--- a/solution.py
+++ b/solution.py
@@ -11,7 +11,7 @@
 EVERY = ("band", "chip", "core")
 TAPS = 9
 LINE = 4
-ORDER = (2, 1, 3, 0)
+ORDER = (1, 3, 2, 0)
 MIB = 1024 * 1024
 TILE = 512
 
@@ -476,7 +476,7 @@
             pltpu.SemaphoreType.DMA((points // TILE,)),
             pltpu.SemaphoreType.DMA((steps,)),
         ],
-        compiler_params=params(56),
+        compiler_params=params(54),
         name="stem",
     )(
         west,
@@ -600,6 +600,7 @@
         jnp.broadcast_to(summed[None], part), EVERY, split_axis=0, concat_axis=0, tiled=True,
         axis_index_groups=planes,
     )
+    steps_out = (2, 3, 1)
     held = [lax.ppermute(mine, EVERY, line_pairs(step)) for step in steps_out]
     out_shape = (
         pltpu.HBM((TAPS, channels, width), f32),

time: 211 us -> 209 us (level)
  waiting for transfers between devices: 72.4 us -> 68.9 us
    ppermute x3, waiting for transfers between devices: 18 us -> 15.3 us  [shards(): lax.ppermute(chip_sum, EVERY, line_pairs(step))]
where the time goes in v3:
time: 209 us; the launch traced here: 208 us
  waiting for transfers between devices  68.9 us (33%)
  Pallas kernels  53.9 us (26%)
  starting transfers between devices  36.5 us (17%)
  blocking collectives  30.5 us (15%)
  local copies, waits for them, and re-layouts  6.85 us (3%)
  matrix products  6.62 us (3%)
  other arithmetic  3.73 us (2%)
    all_to_all x1, waiting for transfers between devices, shards(): lax.all_to_all(outgoing.reshape(device_count, slot_count, width), EVERY,...  28.3 us
    all_to_all x1, blocking collectives, shards(): lax.all_to_all(jnp.broadcast_to(summed[None], part), EVERY, split_axis=0,...  16.7 us
    ppermute x3, waiting for transfers between devices, shards(): lax.ppermute(chip_sum, EVERY, line_pairs(step))  15.3 us
    pallas_call x1, Pallas kernels, shards(): pl.pallas_call(stem_kernel, out_shape=(pltpu.HBM((3, half_rows, half_cols...  14.1 us
    all_to_all x1, blocking collectives, shards(): lax.all_to_all(line_sum, EVERY, split_axis=0, concat_axis=0, tiled=True,...  13.8 us
    pallas_call x1, Pallas kernels, shards(): pl.pallas_call(gradients_kernel, out_shape=(jax.ShapeDtypeStruct(quarter_...  13.1 us
    ppermute x3, waiting for transfers between devices, shards(): held = [lax.ppermute(mine, EVERY, line_pairs(step)) for step in steps_out]  12.1 us
    pallas_call x2, Pallas kernels, edge_call(): pl.pallas_call(functools.partial(edge_kernel, side), out_shape=(pltpu.HBM...  10.3 us
  transfers between devices with their start and end apart: 19, of which 10 were waited for; matrix products, arithmetic and copies ran while one was open for 7% of the time, Pallas kernels for 8%

profile of v3, /device:TPU:1, one launch (start us, length us, event | category | flops | bytes accessed | tf_op | source)
XLA Modules:
  0.0 208.2 jit_solution(12793559069433354084)
XLA Ops:
  1.4 5.8 %collective-permute-start.2 = (bf16[1,1,474]{2,1,0:T(2,128)(2,1)S(1)}, bf16[1,1,474]{2,1,0:T(2,128)(2,1)S(1)}, u32[]{:S(2)}, u32[]{:S(2)}) collective-permute-start(bf16[1,1,474]{2,1,0:T(2,128)(2,1)S(1)} %slice.11), channel_id=1, source_target_pairs={{0,9},{1,10},{2,11},{3,12},{4,13},{5,14},{6,15},{7,8},{8,17},{9,18... | collective-permute-start | bytes 2852 | tf_op jit(solution)/shard_map/ppermute | solution.py:439
  8.1 3.5 %collective-permute-start.1 = (bf16[1,64,474]{2,1,0:T(8,128)(2,1)S(1)}, bf16[1,64,474]{2,1,0:T(8,128)(2,1)S(1)}, u32[]{:S(2)}, u32[]{:S(2)}) collective-permute-start(bf16[1,64,474]{2,1,0:T(8,128)(2,1)S(1)} %slice.10), channel_id=1, source_target_pairs={{0,8},{8,16},{16,24},{24,32},{32,40},{40,48},{48,56},{56,64},{64,7... | collective-permute-start | bytes 182024 | tf_op jit(solution)/shard_map/ppermute | solution.py:438
  17.7 14.1 %stem.1 = (bf16[3,32,32,512]{3,2,1,0:T(8,128)(2,1)}, bf16[3,33,32,512]{3,2,1,0:T(8,128)(2,1)}, f32[1024,512]{1,0:T(8,128)}, bf16[2048,512]{1,0:T(8,128)(2,1)}) custom-call(bf16[64,1,474]{2,1,0:T(2,128)(2,1)} %copy-done.13, bf16[1,64,474]{2,1,0:T(8,128)(2,1)} %copy-done.14, bf16[1,1,474]{2,1,0:T(2,128)(2,1)} %copy-done.16, f32[1,512]{1,0:T(1,128)} %bitcast.25, ...), custom_call_target="tpu_custom_call" | custom-call | tf_op jit(solution)/shard_map/stem/pallas_call | solution.py:453
  31.8 8.0 %all-to-all-start = ((bf16[128,16,512]{2,1,0:T(8,128)(2,1)}), bf16[128,16,512]{2,1,0:T(8,128)(2,1)S(1)}, u32[]{:S(2)}, u32[]{:S(2)}) async-start(bf16[128,16,512]{2,1,0:T(8,128)(2,1)} %bitcast.24), calls=%async_computation | async-start | bytes 4194304 | tf_op jit(solution)/shard_map/all_to_all | solution.py:491
  42.0 28.3 %all-to-all-done = bf16[128,16,512]{2,1,0:T(8,128)(2,1)S(1)} async-done(((bf16[128,16,512]{2,1,0:T(8,128)(2,1)}), bf16[128,16,512]{2,1,0:T(8,128)(2,1)S(1)}, u32[]{:S(2)}, u32[]{:S(2)}) %all-to-all-start) | async-done | bytes 2097184 | tf_op jit(solution)/shard_map/all_to_all | solution.py:491
  70.3 5.2 %edge_back.1 = bf16[2048,512]{1,0:T(8,128)(2,1)} custom-call(bf16[512,512]{1,0:T(8,128)(2,1)S(1)} %copy-done.3, s32[1,2048]{1,0:T(1,128)S(1)} %broadcast_in_dim_reshape.3.dst_ref, bf16[320,512]{1,0:T(8,128)(2,1)S(1)} %convolution_convert_fusion.3.agg_ref, bf16[2048,512]{1,0:T(8,128)(2,1)S(1)} %bitcast.20), custom_call_target="tpu_custom_call" | custom-call | flops 2147483648 | bytes 8388608 | tf_op jit(solution)/shard_map/edge_back/pallas_call | solution.py:516
  75.6 5.5 %all-to-all-start.1 = ((bf16[128,16,512]{2,1,0:T(8,128)(2,1)}), bf16[128,16,512]{2,1,0:T(8,128)(2,1)}, u32[]{:S(2)}, u32[]{:S(2)}) async-start(bf16[128,16,512]{2,1,0:T(8,128)(2,1)} %bitcast.23), calls=%async_computation.1 | async-start | bytes 4194304 | tf_op jit(solution)/shard_map/all_to_all | solution.py:531
  81.6 9.6 %flip.1.patches_hbm = bf16[9,512,1024]{2,1,0:T(8,128)(2,1)} custom-call(bf16[3,32,32,512]{3,2,1,0:T(8,128)(2,1)} %get-tuple-element.45.even_ref, bf16[3,33,32,512]{3,2,1,0:T(8,128)(2,1)} %get-tuple-element.46.odd_ref), custom_call_target="tpu_custom_call" | custom-call | bytes 16777216 | tf_op jit(solution)/shard_map/flip/pallas_call | solution.py:496
  91.2 5.1 %edge_side.1 = (bf16[2048,512]{1,0:T(8,128)(2,1)}, bf16[2048,512]{1,0:T(8,128)(2,1)}) custom-call(bf16[512,512]{1,0:T(8,128)(2,1)S(1)} %copy-done.4, s32[1,2048]{1,0:T(1,128)S(1)} %broadcast_in_dim_reshape.3.dst_ref, bf16[320,512]{1,0:T(8,128)(2,1)S(1)} %convolution_convert_fusion.3.agg_ref, bf16[2048,512]{1,0:T(8,128)(2,1)S(1)} %bitcast.21), custom_call_target="tpu_custom_call" | custom-call | flops 2147483648 | bytes 8388608 | tf_op jit(solution)/shard_map/edge_side/pallas_call | solution.py:516
  96.3 2.5 %fusion.2 = bf16[320,512]{1,0:T(8,128)(2,1)S(1)} fusion(bf16[2048,512]{1,0:T(8,128)(2,1)} %get-tuple-element.39, s32[2048]{0:T(1024)S(1)} %eq.19), kind=kOutput, calls=%fused_computation.8 | convolution fusion | flops 671907840 | bytes 2433024 | tf_op jit(solution)/shard_map/dot_general | solution.py:20
  101.8 9.7 %all-to-all-done.1 = bf16[128,16,512]{2,1,0:T(8,128)(2,1)} async-done(((bf16[128,16,512]{2,1,0:T(8,128)(2,1)}), bf16[128,16,512]{2,1,0:T(8,128)(2,1)}, u32[]{:S(2)}, u32[]{:S(2)}) %all-to-all-start.1) | async-done | bytes 2097184 | tf_op jit(solution)/shard_map/all_to_all | solution.py:531
  111.5 13.1 %gradients.1 = (bf16[11,128,256]{2,1,0:T(8,128)(2,1)S(1)}, bf16[11,128,256]{2,1,0:T(8,128)(2,1)S(1)}, bf16[11,128,256]{2,1,0:T(8,128)(2,1)}, bf16[11,128,256]{2,...) custom-call(s32[4]{0:T(128)S(1)} %broadcast_select_fusion.2.where_re, ...), custom_call_target="tpu_custom_call" | custom-call | tf_op jit(solution)/shard_map/gradients/pallas_call | solution.py:553
  126.3 1.6 collective-permute-done.3
  131.3 2.4 %collective-permute-start.8 = (bf16[11,128,256]{2,1,0:T(8,128)(2,1)S(1)}, bf16[11,128,256]{2,1,0:T(8,128)(2,1)S(1)}, u32[]{:S(2)}, u32[]{:S(2)}) collective-permute-start(bf16[11,128,256]{2,1,0:T(8,128)(2,1)S(1)} %add_convert_fusion), channel_id=1, source_target_pairs={{0,6},{1,97},{2,0},{3,99},{4,2},{5,101},{6,4},{7,103},{8,14},{9,10... | collective-permute-start | bytes 2162696 | tf_op jit(solution)/shard_map/ppermute | solution.py:581
  133.7 7.6 %collective-permute-done.9.three_ref = bf16[11,128,256]{2,1,0:T(8,128)(2,1)S(1)} collective-permute-done((bf16[11,128,256]{2,1,0:T(8,128)(2,1)S(1)}, bf16[11,128,256]{2,1,0:T(8,128)(2,1)S(1)}, u32[]{:S(2)}, u32[]{:S(2)}) %collective-permute-start.9) | collective-permute-done | bytes 720928 | tf_op jit(solution)/shard_map/ppermute | solution.py:581
  141.4 7.7 %collective-permute-done.6.one_ref = bf16[11,128,256]{2,1,0:T(8,128)(2,1)S(1)} collective-permute-done((bf16[11,128,256]{2,1,0:T(8,128)(2,1)S(1)}, bf16[11,128,256]{2,1,0:T(8,128)(2,1)S(1)}, u32[]{:S(2)}, u32[]{:S(2)}) %collective-permute-start.6) | collective-permute-done | bytes 720928 | tf_op jit(solution)/shard_map/ppermute | solution.py:581
  149.5 13.8 %all_to_all.20 = bf16[16,11,16,128]{3,2,1,0:T(8,128)(2,1)S(1)} all-to-all(bf16[16,11,16,128]{3,2,1,0:T(8,128)(2,1)S(1)} %line_sum.1), channel_id=1, replica_groups={{0,8,16,24,32,40,48,56,64,72,80,88,96,104,112,120},{1,9,17,25,3,11,19,2..., dimensions={0} | all-to-all | bytes 1441792 | tf_op jit(solution)/shard_map/all_to_all | solution.py:595
  163.5 16.7 %all_to_all.21.refs_0_ = bf16[16,11,16,128]{3,2,1,0:T(8,128)(2,1)S(1)} all-to-all(bf16[16,11,16,128]{3,2,1,0:T(8,128)(2,1)S(1)} %broadcast_in_dim.16), channel_id=1, replica_groups={{0,8,16,24,32,40,48,56,64,72,80,88,96,104,112,120},{1,9,17,25,3,11,19,2..., dimensions={0} | all-to-all | bytes 1441792 | tf_op jit(solution)/shard_map/all_to_all | solution.py:599
  180.2 1.4 collective-permute-start.11
  181.6 1.6 collective-permute-start.10
  184.6 2.3 %final_own.1 = (f32[9,474,512]{2,1,0:T(8,128)}, f32[1,512]{1,0:T(1,128)}, f32[512,512]{1,0:T(8,128)}, f32[512,512]{1,0:T(8,128)}) custom-call(s32[4]{0:T(128)S(1)} %broadcast_select_fusion.2.where_ref, bf16[16,11,16,128]{3,2,1,0:T(8,128)(2,1)S(1)} %all_to_all.21.refs_0_, bf16[16,11,16,128]{3,2,1,0:T(8,128)(2,1)S(1)} %collective-permute-done.11.refs_1_), custom_call_target="tpu_custom_call" | custom-call | bytes 4194304 | tf_op jit(solution)/shard_map/final_own/pallas_call | solution.py:614
  186.9 6.6 %collective-permute-done.10.refs_0_ = bf16[16,11,16,128]{3,2,1,0:T(8,128)(2,1)S(1)} collective-permute-done((bf16[16,11,16,128]{3,2,1,0:T(8,128)(2,1)S(1)}, bf16[16,11,16,128]{3,2,1,0:T(8,128)(2,1)S(1)}, u32[]{:S(2)}, u32[]{:S(2)}) %collective-permute-start.10) | collective-permute-done | bytes 720928 | tf_op jit(solution)/shard_map/ppermute | solution.py:604
  194.5 5.4 %collective-permute-done.14.refs_2_ = bf16[16,11,16,128]{3,2,1,0:T(8,128)(2,1)S(1)} collective-permute-done((bf16[16,11,16,128]{3,2,1,0:T(8,128)(2,1)S(1)}, bf16[16,11,16,128]{3,2,1,0:T(8,128)(2,1)S(1)}, u32[]{:S(2)}, u32[]{:S(2)}) %collective-permute-start.14) | collective-permute-done | bytes 720928 | tf_op jit(solution)/shard_map/ppermute | solution.py:604
  204.0 4.0 %final_line.1 = (f32[9,474,512]{2,1,0:T(8,128)}, f32[1,512]{1,0:T(1,128)}, f32[512,512]{1,0:T(8,128)}, f32[512,512]{1,0:T(8,128)}) custom-call(s32[4]{0:T(128)S(1)} %broadcast_select_fusion.2.where_ref, bf16[16,11,16,128]{3,2,1,0:T(8,128)(2,1)S(1)} %collective-permute-done.10.refs_0_, ...), custom_call_target="tpu_custom_call", output_to_operand_aliasing={{0}: (7, {}), {1}: (8, {}), {2}: (9, {}), {3}: (10, {})} | custom-call | bytes 12582912 | tf_op jit(solution)/shard_map/final_line/pallas_call | solution.py:614
  (85 shorter events, 25.4 us)
Async XLA Ops:
  0.6 40.0 %copy-start = (bf16[512,512]{1,0:T(8,128)(2,1)S(1)}, bf16[512,512]{1,0:T(8,128)(2,1)}, u32[]{:S(2)}) copy-start(bf16[512,512]{1,0:T(8,128)(2,1)} %param.13) | copy-start | bytes 1572868
  1.4 15.6 %collective-permute-start.2 = (bf16[1,1,474]{2,1,0:T(2,128)(2,1)S(1)}, bf16[1,1,474]{2,1,0:T(2,128)(2,1)S(1)}, u32[]{:S(2)}, u32[]{:S(2)}) collective-permute-start(bf16[1,1,474]{2,1,0:T(2,128)(2,1)S(1)} %slice.11), channel_id=1, source_target_pairs={{0,9},{1,10},{2,11},{3,12},{4,13},{5,14},{6,15},{7,8},{8,17},{9,18... | collective-permute-start | bytes 2852 | tf_op jit(solution)/shard_map/ppermute | solution.py:439
  8.1 8.9 %collective-permute-start.1 = (bf16[1,64,474]{2,1,0:T(8,128)(2,1)S(1)}, bf16[1,64,474]{2,1,0:T(8,128)(2,1)S(1)}, u32[]{:S(2)}, u32[]{:S(2)}) collective-permute-start(bf16[1,64,474]{2,1,0:T(8,128)(2,1)S(1)} %slice.10), channel_id=1, source_target_pairs={{0,8},{8,16},{16,24},{24,32},{32,40},{40,48},{48,56},{56,64},{64,7... | collective-permute-start | bytes 182024 | tf_op jit(solution)/shard_map/ppermute | solution.py:438
  12.8 4.2 %collective-permute-start = (bf16[64,1,474]{2,1,0:T(2,128)(2,1)S(1)}, bf16[64,1,474]{2,1,0:T(2,128)(2,1)S(1)}, u32[]{:S(2)}, u32[]{:S(2)}) collective-permute-start(bf16[64,1,474]{2,1,0:T(2,128)(2,1)S(1)} %slice.9), channel_id=1, source_target_pairs={{0,1},{1,2},{2,3},{3,4},{4,5},{5,6},{6,7},{7,0},{8,9},{9,10},{10,1... | collective-permute-start | bytes 182024 | tf_op jit(solution)/shard_map/ppermute | solution.py:435
  31.8 8.1 %copy-start.15 = (s32[1,128,16]{1,2,0:T(8,128)S(1)}, s32[1,128,16]{1,2,0:T(8,128)}, u32[]{:S(2)}) copy-start(s32[1,128,16]{1,2,0:T(8,128)} %param.15) | copy-start | bytes 24580
  31.8 38.6 %copy-start.3 = (bf16[512,512]{1,0:T(8,128)(2,1)S(1)}, bf16[512,512]{1,0:T(8,128)(2,1)}, u32[]{:S(2)}) copy-start(bf16[512,512]{1,0:T(8,128)(2,1)} %w_ref.3) | copy-start | bytes 1572868
  31.8 38.6 %all-to-all-start = ((bf16[128,16,512]{2,1,0:T(8,128)(2,1)}), bf16[128,16,512]{2,1,0:T(8,128)(2,1)S(1)}, u32[]{:S(2)}, u32[]{:S(2)}) async-start(bf16[128,16,512]{2,1,0:T(8,128)(2,1)} %bitcast.24), calls=%async_computation | async-start | bytes 4194304 | tf_op jit(solution)/shard_map/all_to_all | solution.py:491
  75.6 35.9 %all-to-all-start.1 = ((bf16[128,16,512]{2,1,0:T(8,128)(2,1)}), bf16[128,16,512]{2,1,0:T(8,128)(2,1)}, u32[]{:S(2)}, u32[]{:S(2)}) async-start(bf16[128,16,512]{2,1,0:T(8,128)(2,1)} %bitcast.23), calls=%async_computation.1 | async-start | bytes 4194304 | tf_op jit(solution)/shard_map/all_to_all | solution.py:531
  81.6 9.6 %copy-start.4 = (bf16[512,512]{1,0:T(8,128)(2,1)S(1)}, bf16[512,512]{1,0:T(8,128)(2,1)}, u32[]{:S(2)}) copy-start(bf16[512,512]{1,0:T(8,128)(2,1)} %w_ref.3) | copy-start | bytes 1572868
  124.6 3.3 %collective-permute-start.3 = (bf16[11,128,256]{2,1,0:T(8,128)(2,1)}, bf16[11,128,256]{2,1,0:T(8,128)(2,1)S(1)}, u32[]{:S(2)}, u32[]{:S(2)}) collective-permute-start(bf16[11,128,256]{2,1,0:T(8,128)(2,1)} %get-tuple-element.50), channel_id=1, source_target_pairs={{0,1},{1,0},{2,3},{3,2},{4,5},{5,4},{6,7},{7,6},{8,9},{9,8},{10,11... | collective-permute-start | bytes 2162696 | tf_op jit(solution)/shard_map/ppermute | solution.py:36
  125.8 4.7 %collective-permute-start.5 = (bf16[11,128,256]{2,1,0:T(8,128)(2,1)S(1)}, bf16[11,128,256]{2,1,0:T(8,128)(2,1)S(1)}, u32[]{:S(2)}, u32[]{:S(2)}) collective-permute-start(bf16[11,128,256]{2,1,0:T(8,128)(2,1)S(1)} %get-tuple-element.53), channel_id=1, source_target_pairs={{0,1},{1,0},{2,3},{3,2},{4,5},{5,4},{6,7},{7,6},{8,9},{9,8},{10,11... | collective-permute-start | bytes 2162696 | tf_op jit(solution)/shard_map/ppermute | solution.py:36
  125.9 5.3 %collective-permute-start.7 = (bf16[11,128,256]{2,1,0:T(8,128)(2,1)S(1)}, bf16[11,128,256]{2,1,0:T(8,128)(2,1)S(1)}, u32[]{:S(2)}, u32[]{:S(2)}) collective-permute-start(bf16[11,128,256]{2,1,0:T(8,128)(2,1)S(1)} %get-tuple-element.55), channel_id=1, source_target_pairs={{0,1},{1,0},{2,3},{3,2},{4,5},{5,4},{6,7},{7,6},{8,9},{9,8},{10,11... | collective-permute-start | bytes 2162696 | tf_op jit(solution)/shard_map/ppermute | solution.py:36
  129.3 12.1 %collective-permute-start.9 = (bf16[11,128,256]{2,1,0:T(8,128)(2,1)S(1)}, bf16[11,128,256]{2,1,0:T(8,128)(2,1)S(1)}, u32[]{:S(2)}, u32[]{:S(2)}) collective-permute-start(bf16[11,128,256]{2,1,0:T(8,128)(2,1)S(1)} %add_convert_fusion.2), channel_id=1, source_target_pairs={{0,4},{1,65},{2,6},{3,67},{4,0},{5,69},{6,2},{7,71},{8,12},{9,73},... | collective-permute-start | bytes 2162696 | tf_op jit(solution)/shard_map/ppermute | solution.py:581
  129.8 3.9 %collective-permute-start.4 = (bf16[11,128,256]{2,1,0:T(8,128)(2,1)S(1)}, bf16[11,128,256]{2,1,0:T(8,128)(2,1)S(1)}, u32[]{:S(2)}, u32[]{:S(2)}) collective-permute-start(bf16[11,128,256]{2,1,0:T(8,128)(2,1)S(1)} %copy-done.17), channel_id=1, source_target_pairs={{0,1},{1,0},{2,3},{3,2},{4,5},{5,4},{6,7},{7,6},{8,9},{9,8},{10,11... | collective-permute-start | bytes 2162696 | tf_op jit(solution)/shard_map/ppermute | solution.py:36
  130.5 18.5 %copy-start.2 = (bf16[11,128,256]{2,1,0:T(8,128)(2,1)S(1)}, bf16[11,128,256]{2,1,0:T(8,128)(2,1)}, u32[]{:S(2)}) copy-start(bf16[11,128,256]{2,1,0:T(8,128)(2,1)} %get-tuple-element.47.kept_ref) | copy-start | bytes 2162692
  130.7 18.3 %collective-permute-start.6 = (bf16[11,128,256]{2,1,0:T(8,128)(2,1)S(1)}, bf16[11,128,256]{2,1,0:T(8,128)(2,1)S(1)}, u32[]{:S(2)}, u32[]{:S(2)}) collective-permute-start(bf16[11,128,256]{2,1,0:T(8,128)(2,1)S(1)} %add_convert_fusion.1), channel_id=1, source_target_pairs={{0,2},{1,33},{2,4},{3,35},{4,6},{5,37},{6,0},{7,39},{8,10},{9,41},... | collective-permute-start | bytes 2162696 | tf_op jit(solution)/shard_map/ppermute | solution.py:581
  131.3 17.7 %collective-permute-start.8 = (bf16[11,128,256]{2,1,0:T(8,128)(2,1)S(1)}, bf16[11,128,256]{2,1,0:T(8,128)(2,1)S(1)}, u32[]{:S(2)}, u32[]{:S(2)}) collective-permute-start(bf16[11,128,256]{2,1,0:T(8,128)(2,1)S(1)} %add_convert_fusion), channel_id=1, source_target_pairs={{0,6},{1,97},{2,0},{3,99},{4,2},{5,101},{6,4},{7,103},{8,14},{9,10... | collective-permute-start | bytes 2162696 | tf_op jit(solution)/shard_map/ppermute | solution.py:581
  180.2 4.4 %collective-permute-start.11 = (bf16[16,11,16,128]{3,2,1,0:T(8,128)(2,1)S(1)}, bf16[16,11,16,128]{3,2,1,0:T(8,128)(2,1)S(1)}, u32[]{:S(2)}, u32[]{:S(2)}) collective-permute-start(bf16[16,11,16,128]{3,2,1,0:T(8,128)(2,1)S(1)} %all_to_all.21.refs_0_), channel_id=1, source_target_pairs={{0,1},{1,0},{2,3},{3,2},{4,5},{5,4},{6,7},{7,6},{8,9},{9,8},{10,11... | collective-permute-start | bytes 2162696 | tf_op jit(solution)/shard_map/ppermute | solution.py:36
  181.6 12.0 %collective-permute-start.10 = (bf16[16,11,16,128]{3,2,1,0:T(8,128)(2,1)S(1)}, bf16[16,11,16,128]{3,2,1,0:T(8,128)(2,1)S(1)}, u32[]{:S(2)}, u32[]{:S(2)}) collective-permute-start(bf16[16,11,16,128]{3,2,1,0:T(8,128)(2,1)S(1)} %all_to_all.21.refs_0_), channel_id=1, source_target_pairs={{0,4},{1,65},{2,6},{3,67},{4,0},{5,69},{6,2},{7,71},{8,12},{9,73},... | collective-permute-start | bytes 2162696 | tf_op jit(solution)/shard_map/ppermute | solution.py:604
  183.2 16.7 %collective-permute-start.14 = (bf16[16,11,16,128]{3,2,1,0:T(8,128)(2,1)S(1)}, bf16[16,11,16,128]{3,2,1,0:T(8,128)(2,1)S(1)}, u32[]{:S(2)}, u32[]{:S(2)}) collective-permute-start(bf16[16,11,16,128]{3,2,1,0:T(8,128)(2,1)S(1)} %all_to_all.21.refs_0_), channel_id=1, source_target_pairs={{0,6},{1,97},{2,0},{3,99},{4,2},{5,101},{6,4},{7,103},{8,14},{9,10... | collective-permute-start | bytes 2162696 | tf_op jit(solution)/shard_map/ppermute | solution.py:604
  184.5 16.7 %collective-permute-start.12 = (bf16[16,11,16,128]{3,2,1,0:T(8,128)(2,1)S(1)}, bf16[16,11,16,128]{3,2,1,0:T(8,128)(2,1)S(1)}, u32[]{:S(2)}, u32[]{:S(2)}) collective-permute-start(bf16[16,11,16,128]{3,2,1,0:T(8,128)(2,1)S(1)} %all_to_all.21.refs_0_), channel_id=1, source_target_pairs={{0,2},{1,33},{2,4},{3,35},{4,6},{5,37},{6,0},{7,39},{8,10},{9,41},... | collective-permute-start | bytes 2162696 | tf_op jit(solution)/shard_map/ppermute | solution.py:604
  193.6 7.7 %collective-permute-start.13 = (bf16[16,11,16,128]{3,2,1,0:T(8,128)(2,1)S(1)}, bf16[16,11,16,128]{3,2,1,0:T(8,128)(2,1)S(1)}, u32[]{:S(2)}, u32[]{:S(2)}) collective-permute-start(bf16[16,11,16,128]{3,2,1,0:T(8,128)(2,1)S(1)} %collective-permute-done.10.refs_0_), channel_id=1, source_target_pairs={{0,1},{1,0},{2,3},{3,2},{4,5},{5,4},{6,7},{7,6},{8,9},{9,8},{10,11... | collective-permute-start | bytes 2162696 | tf_op jit(solution)/shard_map/ppermute | solution.py:36
  199.8 3.1 %collective-permute-start.15 = (bf16[16,11,16,128]{3,2,1,0:T(8,128)(2,1)S(1)}, bf16[16,11,16,128]{3,2,1,0:T(8,128)(2,1)S(1)}, u32[]{:S(2)}, u32[]{:S(2)}) collective-permute-start(bf16[16,11,16,128]{3,2,1,0:T(8,128)(2,1)S(1)} %collective-permute-done.14.refs_2_), channel_id=1, source_target_pairs={{0,1},{1,0},{2,3},{3,2},{4,5},{5,4},{6,7},{7,6},{8,9},{9,8},{10,11... | collective-permute-start | bytes 2162696 | tf_op jit(solution)/shard_map/ppermute | solution.py:36
  201.2 2.8 %collective-permute-start.16 = (bf16[16,11,16,128]{3,2,1,0:T(8,128)(2,1)S(1)}, bf16[16,11,16,128]{3,2,1,0:T(8,128)(2,1)S(1)}, u32[]{:S(2)}, u32[]{:S(2)}) collective-permute-start(bf16[16,11,16,128]{3,2,1,0:T(8,128)(2,1)S(1)} %collective-permute-done.12.refs_4_), channel_id=1, source_target_pairs={{0,1},{1,0},{2,3},{3,2},{4,5},{5,4},{6,7},{7,6},{8,9},{9,8},{10,11... | collective-permute-start | bytes 2162696 | tf_op jit(solution)/shard_map/ppermute | solution.py:36
  (13 other events, 38.4 us)

commit v4 on v3

--- a/solution.py
+++ b/solution.py
@@ -567,7 +567,7 @@
             pltpu.SemaphoreType.DMA((2,)),
             pltpu.SemaphoreType.DMA((2, LINE)),
         ],
-        compiler_params=params(51),
+        compiler_params=params(49),
         name="gradients",
     )(where, source_row, returned, slope, grad_edge, grad_node, patches)
 

time: 209 us -> 208 us (level)
  no operation moved by 1% of the time
where the time goes in v4:
time: 208 us
  waiting for transfers between devices  68.6 us (33%)
  Pallas kernels  53.8 us (26%)
  starting transfers between devices  36.5 us (18%)
  blocking collectives  30.5 us (15%)
  local copies, waits for them, and re-layouts  6.84 us (3%)
  matrix products  6.62 us (3%)
  other arithmetic  3.73 us (2%)
    all_to_all x1, waiting for transfers between devices, shards(): lax.all_to_all(outgoing.reshape(device_count, slot_count, width), EVERY,...  28.3 us
    all_to_all x1, blocking collectives, shards(): lax.all_to_all(jnp.broadcast_to(summed[None], part), EVERY, split_axis=0,...  16.7 us
    ppermute x3, waiting for transfers between devices, shards(): lax.ppermute(chip_sum, EVERY, line_pairs(step))  15.3 us
    pallas_call x1, Pallas kernels, shards(): pl.pallas_call(stem_kernel, out_shape=(pltpu.HBM((3, half_rows, half_cols...  14.1 us
    all_to_all x1, blocking collectives, shards(): lax.all_to_all(line_sum, EVERY, split_axis=0, concat_axis=0, tiled=True,...  13.8 us
    pallas_call x1, Pallas kernels, shards(): pl.pallas_call(gradients_kernel, out_shape=(jax.ShapeDtypeStruct(quarter_...  13 us
    ppermute x3, waiting for transfers between devices, shards(): held = [lax.ppermute(mine, EVERY, line_pairs(step)) for step in steps_out]  12.1 us
    pallas_call x2, Pallas kernels, edge_call(): pl.pallas_call(functools.partial(edge_kernel, side), out_shape=(pltpu.HBM...  10.3 us
  transfers between devices with their start and end apart: 19, of which 10 were waited for; matrix products, arithmetic and copies ran while one was open for 7% of the time, Pallas kernels for 8%

profile of v4, /device:TPU:1, one launch (start us, length us, event | category | flops | bytes accessed | tf_op | source)
XLA Modules:
  0.0 207.8 jit_solution(7205993202645188450)
XLA Ops:
  1.4 5.8 %collective-permute-start.2 = (bf16[1,1,474]{2,1,0:T(2,128)(2,1)S(1)}, bf16[1,1,474]{2,1,0:T(2,128)(2,1)S(1)}, u32[]{:S(2)}, u32[]{:S(2)}) collective-permute-start(bf16[1,1,474]{2,1,0:T(2,128)(2,1)S(1)} %slice.11), channel_id=1, source_target_pairs={{0,9},{1,10},{2,11},{3,12},{4,13},{5,14},{6,15},{7,8},{8,17},{9,18... | collective-permute-start | bytes 2852 | tf_op jit(solution)/shard_map/ppermute | solution.py:439
  8.1 3.5 %collective-permute-start.1 = (bf16[1,64,474]{2,1,0:T(8,128)(2,1)S(1)}, bf16[1,64,474]{2,1,0:T(8,128)(2,1)S(1)}, u32[]{:S(2)}, u32[]{:S(2)}) collective-permute-start(bf16[1,64,474]{2,1,0:T(8,128)(2,1)S(1)} %slice.10), channel_id=1, source_target_pairs={{0,8},{8,16},{16,24},{24,32},{32,40},{40,48},{48,56},{56,64},{64,7... | collective-permute-start | bytes 182024 | tf_op jit(solution)/shard_map/ppermute | solution.py:438
  17.7 14.1 %stem.1 = (bf16[3,32,32,512]{3,2,1,0:T(8,128)(2,1)}, bf16[3,33,32,512]{3,2,1,0:T(8,128)(2,1)}, f32[1024,512]{1,0:T(8,128)}, bf16[2048,512]{1,0:T(8,128)(2,1)}) custom-call(bf16[64,1,474]{2,1,0:T(2,128)(2,1)} %copy-done.12, bf16[1,64,474]{2,1,0:T(8,128)(2,1)} %copy-done.13, bf16[1,1,474]{2,1,0:T(2,128)(2,1)} %copy-done.15, f32[1,512]{1,0:T(1,128)} %bitcast.25, ...), custom_call_target="tpu_custom_call" | custom-call | tf_op jit(solution)/shard_map/stem/pallas_call | solution.py:453
  31.8 8.0 %all-to-all-start = ((bf16[128,16,512]{2,1,0:T(8,128)(2,1)}), bf16[128,16,512]{2,1,0:T(8,128)(2,1)S(1)}, u32[]{:S(2)}, u32[]{:S(2)}) async-start(bf16[128,16,512]{2,1,0:T(8,128)(2,1)} %bitcast.24), calls=%async_computation | async-start | bytes 4194304 | tf_op jit(solution)/shard_map/all_to_all | solution.py:491
  42.0 28.3 %all-to-all-done = bf16[128,16,512]{2,1,0:T(8,128)(2,1)S(1)} async-done(((bf16[128,16,512]{2,1,0:T(8,128)(2,1)}), bf16[128,16,512]{2,1,0:T(8,128)(2,1)S(1)}, u32[]{:S(2)}, u32[]{:S(2)}) %all-to-all-start) | async-done | bytes 2097184 | tf_op jit(solution)/shard_map/all_to_all | solution.py:491
  70.3 5.2 %edge_back.1 = bf16[2048,512]{1,0:T(8,128)(2,1)} custom-call(bf16[512,512]{1,0:T(8,128)(2,1)S(1)} %copy-done.3, s32[1,2048]{1,0:T(1,128)S(1)} %broadcast_in_dim_reshape.3.dst_ref, bf16[320,512]{1,0:T(8,128)(2,1)S(1)} %convolution_convert_fusion.3.agg_ref, bf16[2048,512]{1,0:T(8,128)(2,1)S(1)} %bitcast.20), custom_call_target="tpu_custom_call" | custom-call | flops 2147483648 | bytes 8388608 | tf_op jit(solution)/shard_map/edge_back/pallas_call | solution.py:516
  75.6 5.5 %all-to-all-start.1 = ((bf16[128,16,512]{2,1,0:T(8,128)(2,1)}), bf16[128,16,512]{2,1,0:T(8,128)(2,1)}, u32[]{:S(2)}, u32[]{:S(2)}) async-start(bf16[128,16,512]{2,1,0:T(8,128)(2,1)} %bitcast.23), calls=%async_computation.1 | async-start | bytes 4194304 | tf_op jit(solution)/shard_map/all_to_all | solution.py:531
  81.6 9.6 %flip.1.patches_hbm = bf16[9,512,1024]{2,1,0:T(8,128)(2,1)} custom-call(bf16[3,32,32,512]{3,2,1,0:T(8,128)(2,1)} %get-tuple-element.45.even_ref, bf16[3,33,32,512]{3,2,1,0:T(8,128)(2,1)} %get-tuple-element.46.odd_ref), custom_call_target="tpu_custom_call" | custom-call | bytes 16777216 | tf_op jit(solution)/shard_map/flip/pallas_call | solution.py:496
  91.2 5.1 %edge_side.1 = (bf16[2048,512]{1,0:T(8,128)(2,1)}, bf16[2048,512]{1,0:T(8,128)(2,1)}) custom-call(bf16[512,512]{1,0:T(8,128)(2,1)S(1)} %copy-done.4, s32[1,2048]{1,0:T(1,128)S(1)} %broadcast_in_dim_reshape.3.dst_ref, bf16[320,512]{1,0:T(8,128)(2,1)S(1)} %convolution_convert_fusion.3.agg_ref, bf16[2048,512]{1,0:T(8,128)(2,1)S(1)} %bitcast.21), custom_call_target="tpu_custom_call" | custom-call | flops 2147483648 | bytes 8388608 | tf_op jit(solution)/shard_map/edge_side/pallas_call | solution.py:516
  96.3 2.5 %fusion.2 = bf16[320,512]{1,0:T(8,128)(2,1)S(1)} fusion(bf16[2048,512]{1,0:T(8,128)(2,1)} %get-tuple-element.39, s32[2048]{0:T(1024)S(1)} %eq.19), kind=kOutput, calls=%fused_computation.8 | convolution fusion | flops 671907840 | bytes 2433024 | tf_op jit(solution)/shard_map/dot_general | solution.py:20
  101.8 9.7 %all-to-all-done.1 = bf16[128,16,512]{2,1,0:T(8,128)(2,1)} async-done(((bf16[128,16,512]{2,1,0:T(8,128)(2,1)}), bf16[128,16,512]{2,1,0:T(8,128)(2,1)}, u32[]{:S(2)}, u32[]{:S(2)}) %all-to-all-start.1) | async-done | bytes 2097184 | tf_op jit(solution)/shard_map/all_to_all | solution.py:531
  111.4 13.0 %gradients.1 = (bf16[11,128,256]{2,1,0:T(8,128)(2,1)S(1)}, bf16[11,128,256]{2,1,0:T(8,128)(2,1)S(1)}, bf16[11,128,256]{2,1,0:T(8,128)(2,1)S(1)}, bf16[11,128,256...) custom-call(s32[4]{0:T(128)S(1)} %broadcast_select_fusion.2.where_re, ...), custom_call_target="tpu_custom_call" | custom-call | tf_op jit(solution)/shard_map/gradients/pallas_call | solution.py:553
  127.5 1.4 add_convert_fusion.2
  130.9 2.4 %collective-permute-start.8 = (bf16[11,128,256]{2,1,0:T(8,128)(2,1)S(1)}, bf16[11,128,256]{2,1,0:T(8,128)(2,1)S(1)}, u32[]{:S(2)}, u32[]{:S(2)}) collective-permute-start(bf16[11,128,256]{2,1,0:T(8,128)(2,1)S(1)} %add_convert_fusion), channel_id=1, source_target_pairs={{0,6},{1,97},{2,0},{3,99},{4,2},{5,101},{6,4},{7,103},{8,14},{9,10... | collective-permute-start | bytes 2162696 | tf_op jit(solution)/shard_map/ppermute | solution.py:581
  133.3 7.6 %collective-permute-done.9.three_ref = bf16[11,128,256]{2,1,0:T(8,128)(2,1)S(1)} collective-permute-done((bf16[11,128,256]{2,1,0:T(8,128)(2,1)S(1)}, bf16[11,128,256]{2,1,0:T(8,128)(2,1)S(1)}, u32[]{:S(2)}, u32[]{:S(2)}) %collective-permute-start.9) | collective-permute-done | bytes 720928 | tf_op jit(solution)/shard_map/ppermute | solution.py:581
  140.9 7.7 %collective-permute-done.6.one_ref = bf16[11,128,256]{2,1,0:T(8,128)(2,1)S(1)} collective-permute-done((bf16[11,128,256]{2,1,0:T(8,128)(2,1)S(1)}, bf16[11,128,256]{2,1,0:T(8,128)(2,1)S(1)}, u32[]{:S(2)}, u32[]{:S(2)}) %collective-permute-start.6) | collective-permute-done | bytes 720928 | tf_op jit(solution)/shard_map/ppermute | solution.py:581
  149.0 13.8 %all_to_all.20 = bf16[16,11,16,128]{3,2,1,0:T(8,128)(2,1)S(1)} all-to-all(bf16[16,11,16,128]{3,2,1,0:T(8,128)(2,1)S(1)} %line_sum.1), channel_id=1, replica_groups={{0,8,16,24,32,40,48,56,64,72,80,88,96,104,112,120},{1,9,17,25,3,11,19,2..., dimensions={0} | all-to-all | bytes 1441792 | tf_op jit(solution)/shard_map/all_to_all | solution.py:595
  163.0 16.7 %all_to_all.21.refs_0_ = bf16[16,11,16,128]{3,2,1,0:T(8,128)(2,1)S(1)} all-to-all(bf16[16,11,16,128]{3,2,1,0:T(8,128)(2,1)S(1)} %broadcast_in_dim.16), channel_id=1, replica_groups={{0,8,16,24,32,40,48,56,64,72,80,88,96,104,112,120},{1,9,17,25,3,11,19,2..., dimensions={0} | all-to-all | bytes 1441792 | tf_op jit(solution)/shard_map/all_to_all | solution.py:599
  179.7 1.4 collective-permute-start.11
  181.1 1.6 collective-permute-start.10
  184.2 2.3 %final_own.1 = (f32[9,474,512]{2,1,0:T(8,128)}, f32[1,512]{1,0:T(1,128)}, f32[512,512]{1,0:T(8,128)}, f32[512,512]{1,0:T(8,128)}) custom-call(s32[4]{0:T(128)S(1)} %broadcast_select_fusion.2.where_ref, bf16[16,11,16,128]{3,2,1,0:T(8,128)(2,1)S(1)} %all_to_all.21.refs_0_, bf16[16,11,16,128]{3,2,1,0:T(8,128)(2,1)S(1)} %collective-permute-done.11.refs_1_), custom_call_target="tpu_custom_call" | custom-call | bytes 4194304 | tf_op jit(solution)/shard_map/final_own/pallas_call | solution.py:614
  186.5 6.6 %collective-permute-done.10.refs_0_ = bf16[16,11,16,128]{3,2,1,0:T(8,128)(2,1)S(1)} collective-permute-done((bf16[16,11,16,128]{3,2,1,0:T(8,128)(2,1)S(1)}, bf16[16,11,16,128]{3,2,1,0:T(8,128)(2,1)S(1)}, u32[]{:S(2)}, u32[]{:S(2)}) %collective-permute-start.10) | collective-permute-done | bytes 720928 | tf_op jit(solution)/shard_map/ppermute | solution.py:604
  194.0 5.4 %collective-permute-done.14.refs_2_ = bf16[16,11,16,128]{3,2,1,0:T(8,128)(2,1)S(1)} collective-permute-done((bf16[16,11,16,128]{3,2,1,0:T(8,128)(2,1)S(1)}, bf16[16,11,16,128]{3,2,1,0:T(8,128)(2,1)S(1)}, u32[]{:S(2)}, u32[]{:S(2)}) %collective-permute-start.14) | collective-permute-done | bytes 720928 | tf_op jit(solution)/shard_map/ppermute | solution.py:604
  203.6 4.0 %final_line.1 = (f32[9,474,512]{2,1,0:T(8,128)}, f32[1,512]{1,0:T(1,128)}, f32[512,512]{1,0:T(8,128)}, f32[512,512]{1,0:T(8,128)}) custom-call(s32[4]{0:T(128)S(1)} %broadcast_select_fusion.2.where_ref, bf16[16,11,16,128]{3,2,1,0:T(8,128)(2,1)S(1)} %collective-permute-done.10.refs_0_, ...), custom_call_target="tpu_custom_call", output_to_operand_aliasing={{0}: (7, {}), {1}: (8, {}), {2}: (9, {}), {3}: (10, {})} | custom-call | bytes 12582912 | tf_op jit(solution)/shard_map/final_line/pallas_call | solution.py:614
  (81 shorter events, 25.3 us)
Async XLA Ops:
  0.6 40.0 %copy-start = (bf16[512,512]{1,0:T(8,128)(2,1)S(1)}, bf16[512,512]{1,0:T(8,128)(2,1)}, u32[]{:S(2)}) copy-start(bf16[512,512]{1,0:T(8,128)(2,1)} %param.13) | copy-start | bytes 1572868
  1.4 15.6 %collective-permute-start.2 = (bf16[1,1,474]{2,1,0:T(2,128)(2,1)S(1)}, bf16[1,1,474]{2,1,0:T(2,128)(2,1)S(1)}, u32[]{:S(2)}, u32[]{:S(2)}) collective-permute-start(bf16[1,1,474]{2,1,0:T(2,128)(2,1)S(1)} %slice.11), channel_id=1, source_target_pairs={{0,9},{1,10},{2,11},{3,12},{4,13},{5,14},{6,15},{7,8},{8,17},{9,18... | collective-permute-start | bytes 2852 | tf_op jit(solution)/shard_map/ppermute | solution.py:439
  8.1 8.9 %collective-permute-start.1 = (bf16[1,64,474]{2,1,0:T(8,128)(2,1)S(1)}, bf16[1,64,474]{2,1,0:T(8,128)(2,1)S(1)}, u32[]{:S(2)}, u32[]{:S(2)}) collective-permute-start(bf16[1,64,474]{2,1,0:T(8,128)(2,1)S(1)} %slice.10), channel_id=1, source_target_pairs={{0,8},{8,16},{16,24},{24,32},{32,40},{40,48},{48,56},{56,64},{64,7... | collective-permute-start | bytes 182024 | tf_op jit(solution)/shard_map/ppermute | solution.py:438
  12.8 4.2 %collective-permute-start = (bf16[64,1,474]{2,1,0:T(2,128)(2,1)S(1)}, bf16[64,1,474]{2,1,0:T(2,128)(2,1)S(1)}, u32[]{:S(2)}, u32[]{:S(2)}) collective-permute-start(bf16[64,1,474]{2,1,0:T(2,128)(2,1)S(1)} %slice.9), channel_id=1, source_target_pairs={{0,1},{1,2},{2,3},{3,4},{4,5},{5,6},{6,7},{7,0},{8,9},{9,10},{10,1... | collective-permute-start | bytes 182024 | tf_op jit(solution)/shard_map/ppermute | solution.py:435
  31.8 8.1 %copy-start.14 = (s32[1,128,16]{1,2,0:T(8,128)S(1)}, s32[1,128,16]{1,2,0:T(8,128)}, u32[]{:S(2)}) copy-start(s32[1,128,16]{1,2,0:T(8,128)} %param.15) | copy-start | bytes 24580
  31.8 38.6 %copy-start.3 = (bf16[512,512]{1,0:T(8,128)(2,1)S(1)}, bf16[512,512]{1,0:T(8,128)(2,1)}, u32[]{:S(2)}) copy-start(bf16[512,512]{1,0:T(8,128)(2,1)} %w_ref.3) | copy-start | bytes 1572868
  31.8 38.6 %all-to-all-start = ((bf16[128,16,512]{2,1,0:T(8,128)(2,1)}), bf16[128,16,512]{2,1,0:T(8,128)(2,1)S(1)}, u32[]{:S(2)}, u32[]{:S(2)}) async-start(bf16[128,16,512]{2,1,0:T(8,128)(2,1)} %bitcast.24), calls=%async_computation | async-start | bytes 4194304 | tf_op jit(solution)/shard_map/all_to_all | solution.py:491
  75.6 35.9 %all-to-all-start.1 = ((bf16[128,16,512]{2,1,0:T(8,128)(2,1)}), bf16[128,16,512]{2,1,0:T(8,128)(2,1)}, u32[]{:S(2)}, u32[]{:S(2)}) async-start(bf16[128,16,512]{2,1,0:T(8,128)(2,1)} %bitcast.23), calls=%async_computation.1 | async-start | bytes 4194304 | tf_op jit(solution)/shard_map/all_to_all | solution.py:531
  81.5 9.6 %copy-start.4 = (bf16[512,512]{1,0:T(8,128)(2,1)S(1)}, bf16[512,512]{1,0:T(8,128)(2,1)}, u32[]{:S(2)}) copy-start(bf16[512,512]{1,0:T(8,128)(2,1)} %w_ref.3) | copy-start | bytes 1572868
  124.5 3.0 %collective-permute-start.3 = (bf16[11,128,256]{2,1,0:T(8,128)(2,1)S(1)}, bf16[11,128,256]{2,1,0:T(8,128)(2,1)S(1)}, u32[]{:S(2)}, u32[]{:S(2)}) collective-permute-start(bf16[11,128,256]{2,1,0:T(8,128)(2,1)S(1)} %get-tuple-element.50), channel_id=1, source_target_pairs={{0,1},{1,0},{2,3},{3,2},{4,5},{5,4},{6,7},{7,6},{8,9},{9,8},{10,11... | collective-permute-start | bytes 2162696 | tf_op jit(solution)/shard_map/ppermute | solution.py:36
  125.7 4.4 %collective-permute-start.5 = (bf16[11,128,256]{2,1,0:T(8,128)(2,1)S(1)}, bf16[11,128,256]{2,1,0:T(8,128)(2,1)S(1)}, u32[]{:S(2)}, u32[]{:S(2)}) collective-permute-start(bf16[11,128,256]{2,1,0:T(8,128)(2,1)S(1)} %get-tuple-element.53), channel_id=1, source_target_pairs={{0,1},{1,0},{2,3},{3,2},{4,5},{5,4},{6,7},{7,6},{8,9},{9,8},{10,11... | collective-permute-start | bytes 2162696 | tf_op jit(solution)/shard_map/ppermute | solution.py:36
  125.8 4.9 %collective-permute-start.7 = (bf16[11,128,256]{2,1,0:T(8,128)(2,1)S(1)}, bf16[11,128,256]{2,1,0:T(8,128)(2,1)S(1)}, u32[]{:S(2)}, u32[]{:S(2)}) collective-permute-start(bf16[11,128,256]{2,1,0:T(8,128)(2,1)S(1)} %get-tuple-element.55), channel_id=1, source_target_pairs={{0,1},{1,0},{2,3},{3,2},{4,5},{5,4},{6,7},{7,6},{8,9},{9,8},{10,11... | collective-permute-start | bytes 2162696 | tf_op jit(solution)/shard_map/ppermute | solution.py:36
  128.8 12.1 %collective-permute-start.9 = (bf16[11,128,256]{2,1,0:T(8,128)(2,1)S(1)}, bf16[11,128,256]{2,1,0:T(8,128)(2,1)S(1)}, u32[]{:S(2)}, u32[]{:S(2)}) collective-permute-start(bf16[11,128,256]{2,1,0:T(8,128)(2,1)S(1)} %add_convert_fusion.2), channel_id=1, source_target_pairs={{0,4},{1,65},{2,6},{3,67},{4,0},{5,69},{6,2},{7,71},{8,12},{9,73},... | collective-permute-start | bytes 2162696 | tf_op jit(solution)/shard_map/ppermute | solution.py:581
  129.4 3.9 %collective-permute-start.4 = (bf16[11,128,256]{2,1,0:T(8,128)(2,1)S(1)}, bf16[11,128,256]{2,1,0:T(8,128)(2,1)S(1)}, u32[]{:S(2)}, u32[]{:S(2)}) collective-permute-start(bf16[11,128,256]{2,1,0:T(8,128)(2,1)S(1)} %get-tuple-element.51), channel_id=1, source_target_pairs={{0,1},{1,0},{2,3},{3,2},{4,5},{5,4},{6,7},{7,6},{8,9},{9,8},{10,11... | collective-permute-start | bytes 2162696 | tf_op jit(solution)/shard_map/ppermute | solution.py:36
  130.1 18.5 %copy-start.2 = (bf16[11,128,256]{2,1,0:T(8,128)(2,1)S(1)}, bf16[11,128,256]{2,1,0:T(8,128)(2,1)}, u32[]{:S(2)}) copy-start(bf16[11,128,256]{2,1,0:T(8,128)(2,1)} %get-tuple-element.47.kept_ref) | copy-start | bytes 2162692
  130.3 18.3 %collective-permute-start.6 = (bf16[11,128,256]{2,1,0:T(8,128)(2,1)S(1)}, bf16[11,128,256]{2,1,0:T(8,128)(2,1)S(1)}, u32[]{:S(2)}, u32[]{:S(2)}) collective-permute-start(bf16[11,128,256]{2,1,0:T(8,128)(2,1)S(1)} %add_convert_fusion.1), channel_id=1, source_target_pairs={{0,2},{1,33},{2,4},{3,35},{4,6},{5,37},{6,0},{7,39},{8,10},{9,41},... | collective-permute-start | bytes 2162696 | tf_op jit(solution)/shard_map/ppermute | solution.py:581
  130.9 17.7 %collective-permute-start.8 = (bf16[11,128,256]{2,1,0:T(8,128)(2,1)S(1)}, bf16[11,128,256]{2,1,0:T(8,128)(2,1)S(1)}, u32[]{:S(2)}, u32[]{:S(2)}) collective-permute-start(bf16[11,128,256]{2,1,0:T(8,128)(2,1)S(1)} %add_convert_fusion), channel_id=1, source_target_pairs={{0,6},{1,97},{2,0},{3,99},{4,2},{5,101},{6,4},{7,103},{8,14},{9,10... | collective-permute-start | bytes 2162696 | tf_op jit(solution)/shard_map/ppermute | solution.py:581
  179.7 4.5 %collective-permute-start.11 = (bf16[16,11,16,128]{3,2,1,0:T(8,128)(2,1)S(1)}, bf16[16,11,16,128]{3,2,1,0:T(8,128)(2,1)S(1)}, u32[]{:S(2)}, u32[]{:S(2)}) collective-permute-start(bf16[16,11,16,128]{3,2,1,0:T(8,128)(2,1)S(1)} %all_to_all.21.refs_0_), channel_id=1, source_target_pairs={{0,1},{1,0},{2,3},{3,2},{4,5},{5,4},{6,7},{7,6},{8,9},{9,8},{10,11... | collective-permute-start | bytes 2162696 | tf_op jit(solution)/shard_map/ppermute | solution.py:36
  181.1 12.0 %collective-permute-start.10 = (bf16[16,11,16,128]{3,2,1,0:T(8,128)(2,1)S(1)}, bf16[16,11,16,128]{3,2,1,0:T(8,128)(2,1)S(1)}, u32[]{:S(2)}, u32[]{:S(2)}) collective-permute-start(bf16[16,11,16,128]{3,2,1,0:T(8,128)(2,1)S(1)} %all_to_all.21.refs_0_), channel_id=1, source_target_pairs={{0,4},{1,65},{2,6},{3,67},{4,0},{5,69},{6,2},{7,71},{8,12},{9,73},... | collective-permute-start | bytes 2162696 | tf_op jit(solution)/shard_map/ppermute | solution.py:604
  182.7 16.7 %collective-permute-start.14 = (bf16[16,11,16,128]{3,2,1,0:T(8,128)(2,1)S(1)}, bf16[16,11,16,128]{3,2,1,0:T(8,128)(2,1)S(1)}, u32[]{:S(2)}, u32[]{:S(2)}) collective-permute-start(bf16[16,11,16,128]{3,2,1,0:T(8,128)(2,1)S(1)} %all_to_all.21.refs_0_), channel_id=1, source_target_pairs={{0,6},{1,97},{2,0},{3,99},{4,2},{5,101},{6,4},{7,103},{8,14},{9,10... | collective-permute-start | bytes 2162696 | tf_op jit(solution)/shard_map/ppermute | solution.py:604
  184.1 16.7 %collective-permute-start.12 = (bf16[16,11,16,128]{3,2,1,0:T(8,128)(2,1)S(1)}, bf16[16,11,16,128]{3,2,1,0:T(8,128)(2,1)S(1)}, u32[]{:S(2)}, u32[]{:S(2)}) collective-permute-start(bf16[16,11,16,128]{3,2,1,0:T(8,128)(2,1)S(1)} %all_to_all.21.refs_0_), channel_id=1, source_target_pairs={{0,2},{1,33},{2,4},{3,35},{4,6},{5,37},{6,0},{7,39},{8,10},{9,41},... | collective-permute-start | bytes 2162696 | tf_op jit(solution)/shard_map/ppermute | solution.py:604
  193.1 7.7 %collective-permute-start.13 = (bf16[16,11,16,128]{3,2,1,0:T(8,128)(2,1)S(1)}, bf16[16,11,16,128]{3,2,1,0:T(8,128)(2,1)S(1)}, u32[]{:S(2)}, u32[]{:S(2)}) collective-permute-start(bf16[16,11,16,128]{3,2,1,0:T(8,128)(2,1)S(1)} %collective-permute-done.10.refs_0_), channel_id=1, source_target_pairs={{0,1},{1,0},{2,3},{3,2},{4,5},{5,4},{6,7},{7,6},{8,9},{9,8},{10,11... | collective-permute-start | bytes 2162696 | tf_op jit(solution)/shard_map/ppermute | solution.py:36
  199.4 3.1 %collective-permute-start.15 = (bf16[16,11,16,128]{3,2,1,0:T(8,128)(2,1)S(1)}, bf16[16,11,16,128]{3,2,1,0:T(8,128)(2,1)S(1)}, u32[]{:S(2)}, u32[]{:S(2)}) collective-permute-start(bf16[16,11,16,128]{3,2,1,0:T(8,128)(2,1)S(1)} %collective-permute-done.14.refs_2_), channel_id=1, source_target_pairs={{0,1},{1,0},{2,3},{3,2},{4,5},{5,4},{6,7},{7,6},{8,9},{9,8},{10,11... | collective-permute-start | bytes 2162696 | tf_op jit(solution)/shard_map/ppermute | solution.py:36
  200.8 2.8 %collective-permute-start.16 = (bf16[16,11,16,128]{3,2,1,0:T(8,128)(2,1)S(1)}, bf16[16,11,16,128]{3,2,1,0:T(8,128)(2,1)S(1)}, u32[]{:S(2)}, u32[]{:S(2)}) collective-permute-start(bf16[16,11,16,128]{3,2,1,0:T(8,128)(2,1)S(1)} %collective-permute-done.12.refs_4_), channel_id=1, source_target_pairs={{0,1},{1,0},{2,3},{3,2},{4,5},{5,4},{6,7},{7,6},{8,9},{9,8},{10,11... | collective-permute-start | bytes 2162696 | tf_op jit(solution)/shard_map/ppermute | solution.py:36
  (11 other events, 27.2 us)
